TPU v7x, 256 devices: a whole 4x4x8 slice. The times are simulated.
256 devices in a mesh: row: 32 (over z, y_hi, core), col: 8 (over y_lo, x).
Axes of the slice: x: 4, y: 4 (y_hi: 2, y_lo: 2; y = y_hi * 2 + y_lo), z: 8, core: 2. Of those that a mesh axis runs over, the one named last changes fastest.
Arguments:
- queries: bfloat16 [32768, 512], P(('row', 'col')), may hold values from -6 to 6
- keys: bfloat16 [32768, 128], P(('row', 'col')), may hold values from -6 to 6
- values: bfloat16 [32768, 128], P(('row', 'col')), may hold values from -6 to 6
- outputs: bfloat16 [32768, 512], P(('row', 'col')), may hold values from -6 to 6
- out_grad: bfloat16 [32768, 512], P(('row', 'col')), may hold values from -4 to 4
- log_sum_exp: float32 [32768, 4], P(('row', 'col')), may hold values from 2 to 4
- segment_ids: int32 [32768], P(('row', 'col')), may hold values from 0 to 67, never falling along the last dimension, each value on 1 to 17408 neighbouring positions
Outputs:
- grad_queries: bfloat16 [32768, 512], P(('row', 'col'))
- grad_keys: bfloat16 [32768, 128], P(('row', 'col'))
- grad_values: bfloat16 [32768, 128], P(('row', 'col'))
Inputs may be any that keep to these rules, and one draw needn't show every extreme that they name: `segment_ids`: segment numbers never fall along the tokens; each document holds at most 17408 tokens, and one holds exactly that many.
All inputs are finite; a program needn't handle non-finite values.
Results may differ from a plain program's by a relative error of at most 0.0053.
Values may be sent and summed in bfloat16 or wider, within the bound.
A program may use at most 64 MiB of HBM per device.

v0:
```python
import jax
import jax.numpy as jnp
from jax import lax
from jax.sharding import PartitionSpec as P

HD = 128
KVH = 1
GROUP = 4


def block_grads(query_side, key_rows, value_rows, key_pos, key_seg):
    query_heads, dout_heads, lse_t, dot_t, query_pos, query_seg = query_side
    row_count = key_rows.shape[0]
    query_count = query_heads.shape[0]
    kv_heads = query_heads.shape[1]
    group_size = query_heads.shape[2]
    head_dim = query_heads.shape[3]
    scaling = head_dim ** (-0.5)
    key_heads = key_rows.reshape(row_count, kv_heads, head_dim)
    value_heads = value_rows.reshape(row_count, kv_heads, head_dim)
    visible = (key_pos[None, :] <= query_pos[:, None]) & (key_seg[None, :] == query_seg[:, None])
    query_shape = (query_count, kv_heads * group_size * head_dim)
    kv_shape = (row_count, 2 * kv_heads * head_dim)

    def compute(unused):
        scores = (
            jnp.einsum("qhgd,khd->hgqk", query_heads, key_heads, preferred_element_type=jnp.float32)
            * scaling
        )
        attn_probs = jnp.where(visible, jnp.exp(scores - lse_t[..., None]), 0.0)
        dprobs = jnp.einsum(
            "qhgd,khd->hgqk", dout_heads, value_heads, preferred_element_type=jnp.float32
        )
        dscores = attn_probs * (dprobs - dot_t[..., None])
        probs_half = attn_probs.astype(jnp.bfloat16)
        dscores_half = dscores.astype(jnp.bfloat16)
        grad_query = (
            jnp.einsum(
                "hgqk,khd->qhgd", dscores_half, key_heads, preferred_element_type=jnp.float32
            )
            * scaling
        ).reshape(query_shape)
        grad_key = (
            jnp.einsum(
                "hgqk,qhgd->khd", dscores_half, query_heads, preferred_element_type=jnp.float32
            )
            * scaling
        )
        grad_value = jnp.einsum(
            "hgqk,qhgd->khd", probs_half, dout_heads, preferred_element_type=jnp.float32
        )
        grad_kv = jnp.concatenate(
            [grad_key.reshape(row_count, -1), grad_value.reshape(row_count, -1)], 1
        )
        return (grad_query, grad_kv)

    def skipped(unused):
        return (jnp.zeros(query_shape, jnp.float32), jnp.zeros(kv_shape, jnp.float32))

    return lax.cond(jnp.any(visible), compute, skipped, 0)


def over_blocks(query_side, key_rows, value_rows, key_pos, key_seg):
    row_count = key_rows.shape[0]
    step_rows = 512
    step_count = row_count // step_rows
    stacked = (
        key_rows.reshape(step_count, step_rows, -1),
        value_rows.reshape(step_count, step_rows, -1),
        key_pos.reshape(step_count, step_rows),
        key_seg.reshape(step_count, step_rows),
    )
    query_count = query_side[0].shape[0]
    query_width = query_side[0].shape[1] * query_side[0].shape[2] * query_side[0].shape[3]

    def visit(running, key_block):
        grad_query, grad_kv = block_grads(
            query_side, key_block[0], key_block[1], key_block[2], key_block[3]
        )
        return (running + grad_query, grad_kv)

    running, kv_blocks = lax.scan(
        visit, jnp.zeros((query_count, query_width), jnp.float32), stacked
    )
    return (running, kv_blocks.reshape(row_count, -1))


def body(queries, keys, values, outputs, out_grad, log_sum_exp, segment_ids):
    own_tokens = queries.shape[0]
    col_size = lax.axis_size("col")
    row_index = lax.axis_index("row")
    col_index = lax.axis_index("col")
    head_count = KVH * GROUP
    row_dot = jnp.sum(
        (out_grad.astype(jnp.float32) * outputs.astype(jnp.float32)).reshape(
            own_tokens, head_count, HD
        ),
        -1,
    )
    seg_half = segment_ids.astype(jnp.bfloat16)
    query_pos = row_index * col_size * own_tokens + jnp.arange(
        col_size * own_tokens, dtype=jnp.int32
    )
    query_rows, dout_rows, qseg_rows = (
        lax.all_gather(queries, "col", axis=0, tiled=True),
        lax.all_gather(out_grad, "col", axis=0, tiled=True),
        lax.all_gather(seg_half, "col", axis=0, tiled=True),
    )
    lse_rows, dot_rows = (
        lax.all_gather(log_sum_exp, "col", axis=0, tiled=True),
        lax.all_gather(row_dot, "col", axis=0, tiled=True),
    )
    query_count = query_rows.shape[0]
    query_pack = (
        query_rows.reshape(query_count, KVH, GROUP, HD),
        dout_rows.reshape(query_count, KVH, GROUP, HD),
        jnp.transpose(lse_rows.reshape(query_count, KVH, GROUP), (1, 2, 0)),
        jnp.transpose(dot_rows.reshape(query_count, KVH, GROUP), (1, 2, 0)),
        query_pos,
        qseg_rows.astype(jnp.int32),
    )
    pieces = (
        lax.all_gather(keys, "row", axis=0, tiled=True),
        lax.all_gather(values, "row", axis=0, tiled=True),
        lax.all_gather(seg_half, "row", axis=0, tiled=True),
    )
    row_count = pieces[0].shape[0]
    gathered_ids = jnp.arange(row_count, dtype=jnp.int32)
    added, kv_grads = over_blocks(
        query_pack,
        pieces[0],
        pieces[1],
        (gathered_ids // own_tokens * col_size + col_index) * own_tokens
        + gathered_ids % own_tokens,
        pieces[2].astype(jnp.int32),
    )
    kv_mine = lax.psum_scatter(kv_grads, "row", scatter_dimension=0, tiled=True)
    grad_queries = lax.psum_scatter(added, "col", scatter_dimension=0, tiled=True).astype(
        jnp.bfloat16
    )
    kv_width = KVH * HD
    return (
        grad_queries,
        kv_mine[:, :kv_width].astype(jnp.bfloat16),
        kv_mine[:, kv_width:].astype(jnp.bfloat16),
    )


def solution(mesh):
    placed = (
        P(("row", "col"), None),
        P(("row", "col"), None),
        P(("row", "col"), None),
        P(("row", "col"), None),
        P(("row", "col"), None),
        P(("row", "col"), None),
        P(("row", "col")),
    )
    return jax.shard_map(
        body,
        mesh=mesh,
        in_specs=placed,
        out_specs=(P(("row", "col"), None), P(("row", "col"), None), P(("row", "col"), None)),
        check_vma=False,
    )
```

profile of v0, /device:TPU:2, one launch (start us, length us, event | category | flops | bytes accessed | tf_op | source)
XLA Modules:
  0.0 566.8 jit_solution(7502001635527303397)
XLA Ops:
  10.7 17.2 %all-gather.1 = bf16[8,1,128]{2,1,0:T(2,128)(2,1)S(1)} all-gather(bf16[1,1,128]{2,1,0:T(2,128)(2,1)S(1)} %convert_bitcast_fusion), channel_id=1, replica_groups=mesh['row'=32,'col'=8] {'col'}, dimensions={0}, use_global_device_ids=true | all-gather | bytes 2304 | tf_op jit(solution)/shard_map/all_gather | solution.py:107
  27.9 43.1 %all-gather = bf16[32,1,128]{2,1,0:T(2,128)(2,1)S(1)} all-gather(bf16[1,1,128]{2,1,0:T(2,128)(2,1)S(1)} %convert_bitcast_fusion), channel_id=1, replica_groups=mesh['row'=32,'col'=8] {'row'}, dimensions={0}, use_global_device_ids=true | all-gather | bytes 8448 | tf_op jit(solution)/shard_map/all_gather | solution.py:125
  72.4 28.3 %all_gather.31 = f32[1024,4]{1,0:T(8,128)S(1)} all-gather(f32[128,4]{1,0:T(8,128)S(1)} %reduce_sum.9), channel_id=1, replica_groups=mesh['row'=32,'col'=8] {'col'}, dimensions={0}, use_global_device_ids=true | all-gather | bytes 18432 | tf_op jit(solution)/shard_map/all_gather | solution.py:111
  100.9 25.2 %all_gather.28 = f32[1024,4]{0,1:T(4,128)S(1)} all-gather(f32[128,4]{0,1:T(4,128)} %param.16), channel_id=1, replica_groups=mesh['row'=32,'col'=8] {'col'}, dimensions={0}, use_global_device_ids=true | all-gather | bytes 18432 | tf_op jit(solution)/shard_map/all_gather | solution.py:110
  127.7 2.3 copy.27
  130.0 46.7 %all-gather.7.cloned.1.call-done = bf16[4096,128]{1,0:T(8,128)(2,1)} async-done(((bf16[128,128]{1,0:T(8,128)(2,1)}), bf16[4096,128]{1,0:T(8,128)(2,1)}) %all-gather.7.cloned.1.call-update) | async-done | bytes 1048592 | tf_op jit(solution)/shard_map/all_gather | solution.py:123
  176.7 77.0 %all-gather.11.cloned.1.call-done = bf16[4096,128]{1,0:T(8,128)(2,1)} async-done(((bf16[128,128]{1,0:T(8,128)(2,1)}), bf16[4096,128]{1,0:T(8,128)(2,1)}) %all-gather.11.cloned.1.call-update) | async-done | bytes 1048592 | tf_op jit(solution)/shard_map/all_gather | solution.py:124
  253.8 83.4 %while.13 = (s32[]{:T(128)}, f32[1024,512]{0,1:T(8,128)}, f32[8,512,256]{2,1,0:T(8,128)}, s32[8,512]{1,0:T(8,128)S(1)}, s32[8,512]{1,0:T(8,128)S(1)}, /*index=5*...) while((s32[]{:T(128)}, f32[1024,512]{0,1:T(8,128)}, ...), condition=%wide.region_5.6_spmd.clone, body=%wide.region_1.5_spmd.clone.sunk | while | flops 2709193728 | bytes 62335280 | solution.py:82
  256.4 12.5 %conditional.3 = (f32[1024,512]{0,1:T(8,128)S(1)}, f32[1,512,256]{1,2,0:T(8,128)}) conditional(s32[]{:T(128)} %convert_element_type.51, () %tuple.52, (bf16[8,512,128]{2,1,0:T(8,128)(2,1)}, s32[]{:T(128)}, pred[1024,512]{0,1:T(8,128)(4,1)}, bf16[1024,1,4,128]{0,3,2,1:T(8,128)(2,1)S(1)}, f32[1,4,1024]{2,1,0:T(4,128)S(1)}, ...), branch_computations={%region_3.3_spmd, %region_4.4_spmd} | conditional | flops 2706046976 | bytes 53397064 | solution.py:60
  256.5 2.3 fusion.19
  258.7 2.1 fusion.13
  260.8 4.0 fusion.8
  272.8 2.0 fusion.46
  276.5 3.4 select_add_fusion.2
  281.9 2.0 fusion.46
  285.7 3.4 select_add_fusion.2
  294.9 3.4 select_add_fusion.2
  304.1 3.4 select_add_fusion.2
  313.3 3.4 select_add_fusion.2
  322.5 3.4 select_add_fusion.2
  331.7 3.4 select_add_fusion.2
  337.2 2.9 copy.29
  340.7 83.8 %reduce-scatter.3.cloned.1.call-done = f32[128,512]{1,0:T(8,128)} async-done(((f32[1024,512]{1,0:T(8,128)}), f32[128,512]{1,0:T(8,128)}) %reduce-scatter.3.cloned.1.call-update) | async-done | bytes 262160 | tf_op jit(solution)/shard_map/reduce_scatter | solution.py:138
  426.2 132.2 %reduce-scatter.5.cloned.1.call-done = f32[128,256]{1,0:T(8,128)} async-done(((f32[4096,256]{1,0:T(8,128)}), f32[128,256]{1,0:T(8,128)}) %reduce-scatter.5.cloned.1.call-update) | async-done | bytes 131088 | tf_op jit(solution)/shard_map/reduce_scatter | solution.py:137
  (96 shorter events, 60.4 us)
Async XLA Ops:
  7.2 119.0 %all-gather.9.cloned.1.call-start = ((), (), s32[]{:S(2)}) async-start(), calls=%async_computation.3 | async-start | bytes 1179648 | tf_op jit(solution)/shard_map/all_gather | solution.py:105
  7.9 119.8 %all-gather.13.cloned.1.call-start = ((), (), s32[]{:S(2)}) async-start(), calls=%async_computation.5 | async-start | bytes 1179648 | tf_op jit(solution)/shard_map/all_gather | solution.py:106
  8.6 168.1 %all-gather.7.cloned.1.call-start = ((), (), s32[]{:S(2)}) async-start(), calls=%async_computation.2 | async-start | bytes 1081344 | tf_op jit(solution)/shard_map/all_gather | solution.py:123
  9.4 244.4 %all-gather.11.cloned.1.call-start = ((), (), s32[]{:S(2)}) async-start(), calls=%async_computation.4 | async-start | bytes 1081344 | tf_op jit(solution)/shard_map/all_gather | solution.py:124
  10.0 414.6 %reduce-scatter.3.cloned.1.call-start = ((), (), s32[]{:S(2)}) async-start(), calls=%async_computation.6 | async-start | bytes 2359296 | tf_op jit(solution)/shard_map/reduce_scatter | solution.py:138
  256.4 2.3 copy-start
  256.4 2.3 copy-start.1
  340.1 218.3 %reduce-scatter.5.cloned.1.call-start = ((), (), s32[]{:S(2)}) async-start(), calls=%async_computation.7 | async-start | bytes 4325376 | tf_op jit(solution)/shard_map/reduce_scatter | solution.py:137
Sparse Core Ops, SparseCore 0:
  9.8 42.0 all-gather.8
  53.7 40.8 all-gather.12
  97.3 79.3 all-gather.6
  179.4 74.3 all-gather.10
  340.2 84.2 reduce-scatter.2
  428.6 129.7 reduce-scatter.4
where the time goes:
time: 568 us; the launch traced here: 567 us
  waiting for transfers between devices  343 us (60%)
  blocking collectives  114 us (20%)
  other arithmetic  46.7 us (8%)
  local copies, waits for them, and re-layouts  32 us (6%)
  between operations  14.2 us (2%)
  matrix products  11.6 us (2%)
    reduce_scatter x1, waiting for transfers between devices, body(): kv_mine = lax.psum_scatter(kv_grads, 'row', scatter_dimension=0, tiled=True)  132 us
    reduce_scatter x1, waiting for transfers between devices, body(): lax.psum_scatter(added, 'col', scatter_dimension=0, tiled=True)  83.8 us
    all_gather x1, waiting for transfers between devices, body(): lax.all_gather(values, 'row', axis=0, tiled=True)  77 us
    all_gather x1, waiting for transfers between devices, body(): lax.all_gather(keys, 'row', axis=0, tiled=True)  46.7 us
    all_gather x1, blocking collectives, body(): lax.all_gather(seg_half, 'row', axis=0, tiled=True)  43.1 us
    all_gather x1, blocking collectives, body(): lax.all_gather(row_dot, 'col', axis=0, tiled=True)  28.3 us
    all_gather x1, blocking collectives, body(): lax.all_gather(log_sum_exp, 'col', axis=0, tiled=True)  25.2 us
    add x8, other arithmetic, visit(): return (running + grad_query, grad_kv)  25.2 us
  transfers between devices with their start and end apart: 6, of which 4 were waited for; matrix products, arithmetic and copies ran while one was open for 1% of the time, Pallas kernels for 0%

commit v1 on v0

v1 whole, which is shorter than its diff:
```python
import functools
import math

import jax
import jax.numpy as jnp
from jax import lax
from jax.experimental import pallas as pl
from jax.experimental.pallas import tpu as pltpu
from jax.sharding import PartitionSpec as P

MESH = pl.DeviceIdType.MESH
HD = 128
GROUP = 4
NZ, NY, NX, NC = 8, 4, 4, 2
TOK = 128
PIECE = TOK // NZ
ROWS = PIECE * GROUP
NG = NZ * NY * NC
TILE_G = 4
NQT = NG // TILE_G
QT = TILE_G * ROWS
KT = 512
SUB = 128
ROUND = 96
BOTH = TOK - ROUND
NKEY = NZ * NX * TOK
NKT = NKEY // KT
CHUNK = NX * TOK
IDS = 72
STEPS = NQT * NKT + 4
SCALE = HD ** -0.5
LOG2E = math.log2(math.e)
BF = jnp.bfloat16
F32 = jnp.float32


def place():
    row = lax.axis_index("row")
    col = lax.axis_index("col")
    z = row // 4
    y = (row // 2) % 2 * 2 + col // 4
    return z, y, col % 4, row % 2


def device(z, y, x, c):
    return (z * 4 + y // 2 * 2 + c, y % 2 * 4 + x)


class Copies:
    def __init__(self, send, recv):
        self.send, self.recv, self.count, self.all = send, recv, 0, []

    def start(self, src, dst, to):
        i = self.count
        self.count += 1
        copy = pltpu.make_async_remote_copy(
            src_ref=src,
            dst_ref=dst,
            send_sem=self.send.at[i],
            recv_sem=self.recv.at[i],
            device_id=to,
            device_id_type=MESH,
        )
        copy.start()
        self.all.append(copy)
        return copy

    def finish(self):
        for copy in self.all:
            copy.wait_send()


def greet(peers):
    barrier = pltpu.get_barrier_semaphore()
    for peer in peers:
        pl.semaphore_signal(barrier, inc=1, device_id=peer, device_id_type=MESH)
    pl.semaphore_wait(barrier, len(peers))


N_GATHER = 32 + 7 + 7 + 7 + 24 + 4 + 11 + 10


def gather_kernel(
    q_in, k_in, v_in, o_in, do_in, lse_in, seg_in, kv_all, qd_all, st_all, sg_all,
    q_ref, o_ref, do_ref, lse_ref, seg_ref, qd_ref, st_ref, send, recv, local,
):
    z, y, x, c = place()
    xp, xm, xo = (x + 1) % NX, (x + 3) % NX, (x + 2) % NX
    yp, ym, yo = (y + 1) % NY, (y + 3) % NY, (y + 2) % NY
    zp, zm = (z + 1) % NZ, (z + NZ - 1) % NZ
    right, left, across = device(z, y, xp, c), device(z, y, xm, c), device(z, y, xo, c)
    up, down, beyond = device(z, yp, x, c), device(z, ym, x, c), device(z, yo, x, c)
    z_right, z_left = device(zp, y, x, c), device(zm, y, x, c)
    twin = device(z, y, x, 1 - c)
    planes = [(z + d) % NZ for d in range(1, NZ)]
    load = [
        pltpu.make_async_copy(src, dst, local.at[i])
        for i, (src, dst) in enumerate([
            (k_in, kv_all.at[z, x, :, pl.ds(0, HD)]),
            (v_in, kv_all.at[z, x, :, pl.ds(HD, HD)]),
            (q_in, q_ref),
            (do_in, do_ref),
            (o_in, o_ref),
            (lse_in, lse_ref),
            (seg_in, seg_ref),
        ])
    ]
    for copy in load:
        copy.start()
    greet(
        [right, left, across, up, down, beyond, twin] + [device(w, y, x, c) for w in planes]
    )
    copies = Copies(send, recv)
    start = copies.start
    yh, yl = y // 2, y % 2

    def spread(d):
        zb = (z + NZ + d) % NZ
        count = TOK if d == 0 else ROUND
        src = kv_all.at[zb, x, pl.ds(0, count)]
        near[d] = (start(src, src, right), start(src, src, left))

    def pass_on(d):
        zb = (z + NZ + d) % NZ
        count = (TOK if d == 0 else ROUND) // 2
        near[d][0].wait_recv()
        src = kv_all.at[zb, xm, pl.ds(0, count)]
        far[d] = [start(src, src, right)]
        near[d][1].wait_recv()
        src = kv_all.at[zb, xp, pl.ds(count, count)]
        far[d].append(start(src, src, left))

    def ring_a(s):
        if s > 0:
            hops["r", s].wait_recv()
        if s < 4:
            src = kv_all.at[(z + NZ - s) % NZ, x, pl.ds(0, ROUND)]
            hops["r", s + 1] = start(src, src, z_right)
        if 0 < s < 4:
            hops["l", s].wait_recv()
        if s < 3:
            src = kv_all.at[(z + s) % NZ, x, pl.ds(0, ROUND)]
            hops["l", s + 1] = start(src, src, z_left)

    def ring_b(s):
        if s > 0:
            hops["R", s].wait_recv()
        if s < 4:
            src = kv_all.at[(z + NZ - s) % NZ, :, pl.ds(ROUND, BOTH)]
            hops["R", s + 1] = start(src, src, z_right)
        if 0 < s < 4:
            hops["L", s].wait_recv()
        if s < 3:
            src = kv_all.at[(z + s) % NZ, :, pl.ds(ROUND, BOTH)]
            hops["L", s + 1] = start(src, src, z_left)

    def q_send(d):
        w = (z + NZ + d) % NZ
        pieces[d] = start(qd_ref.at[w], qd_all.at[z, yh, c, yl], device(w, y, x, c))

    def q_share(d):
        if d != 0:
            pieces[d].wait_recv()
        src = qd_all.at[(z + NZ - d) % NZ, yh, c, yl]
        q_near[d] = (start(src, src, up), start(src, src, down))

    def q_pass(d):
        zz = (z + NZ - d) % NZ
        q_near[d][0].wait_recv()
        q_near[d][1].wait_recv()
        if steps.index(d) % 2 == 0:
            src = qd_all.at[zz, ym // 2, c, ym % 2]
            q_far.append(start(src, src, up))
        else:
            src = qd_all.at[zz, yp // 2, c, yp % 2]
            q_far.append(start(src, src, down))

    def q_across(yy):
        src = qd_all.at[:, yy // 2, c, yy % 2]
        ends.append(start(src, src, twin))

    near, far, hops, pieces, q_near, q_far, ends = {}, {}, {}, {}, {}, [], []
    steps = [0, 1, -1, 2, -2, 3, -3, 4]
    load[0].wait()
    load[1].wait()
    spread(0)
    ring_a(0)
    load[2].wait()
    load[3].wait()
    for w in range(NZ):
        for h in range(GROUP):
            here = (slice(w * PIECE, (w + 1) * PIECE), slice(h * HD, (h + 1) * HD))
            there = slice(h * PIECE, (h + 1) * PIECE)
            qd_ref[w, 0, there] = q_ref[here]
            qd_ref[w, 1, there] = do_ref[here]
    for d in (1, -1, 2, -2):
        q_send(d)
    qd_all[z, yh, c, yl] = qd_ref[z]
    q_share(0)

    for copy in load[4:]:
        copy.wait()
    sub = lax.broadcasted_iota(jnp.int32, (TOK, TOK), 0)
    lane = lax.broadcasted_iota(jnp.int32, (TOK, TOK), 1)
    dots = []
    for h in range(GROUP):
        cols = slice(h * HD, (h + 1) * HD)
        both = lax.dot_general(
            do_ref[:, cols], o_ref[:, cols], (((1,), (1,)), ((), ())),
            preferred_element_type=F32,
        )
        dots.append(jnp.sum(jnp.where(sub == lane, both, 0.0), axis=0, keepdims=True))
    stats = jnp.concatenate([lse_ref[...]] + dots, axis=0)
    seg = seg_ref[...].astype(F32)
    sg_all[z, x] = seg
    segs = jnp.broadcast_to(seg, (2 * GROUP, TOK))
    sub, block = sub[0:8], lane[0:8] // PIECE
    turned = [
        [a if d == 0 else pltpu.roll(a, d * PIECE, 1) for d in range(NZ)] for a in (stats, segs)
    ]
    for w in range(NZ):
        for i in range(2):
            row = jnp.zeros((8, TOK), F32)
            for d in range(NZ):
                row += jnp.where((block == sub) & ((sub + NZ - w) % NZ == d), turned[i][d], 0.0)
            st_ref[w, i:i + 1, :] = jnp.sum(row, axis=0, keepdims=True)
    small = [
        start(st_ref.at[w], st_all.at[z, yh, c, yl], device(w, y, x, c)) for w in planes
    ]
    sg_ref = sg_all.at[z, x]
    marks = [start(sg_ref, sg_ref, device(w, y, x, c)) for w in planes]
    st_all[z, yh, c, yl] = st_ref[z]

    ring_a(1)
    spread(-1)
    spread(1)
    pass_on(0)
    ring_a(2)
    spread(-2)
    spread(2)
    for d in (3, -3, 4):
        q_send(d)
    for copy in far[0]:
        copy.wait_recv()
    ring_b(0)
    q_share(1)
    q_share(-1)
    pass_on(-1)
    ring_a(3)
    spread(-3)
    spread(3)
    pass_on(1)
    q_share(2)
    q_share(-2)
    q_pass(0)
    q_pass(1)
    ring_b(1)
    pass_on(-2)
    ring_a(4)
    spread(-4)
    q_pass(-1)
    for copy in small + marks:
        copy.wait_recv()
    few = st_all.at[:, yh, c, yl]
    st_y = [start(few, few, to) for to in (up, down, beyond)]
    few = sg_all.at[:, x]
    sg_x = [start(few, few, to) for to in (right, left, across)]
    pass_on(2)
    q_share(3)
    q_share(-3)
    q_share(4)
    q_across(y)
    ring_b(2)
    q_pass(2)
    q_pass(-2)
    pass_on(-3)
    for copy in st_y:
        copy.wait_recv()
    few = st_all.at[:, :, c]
    ends.append(start(few, few, twin))
    pass_on(3)
    ring_b(3)
    q_pass(3)
    q_pass(-3)
    q_pass(4)
    q_across(yp)
    q_across(ym)
    pass_on(-4)
    for copy in q_far:
        copy.wait_recv()
    q_across(yo)
    ring_b(4)
    for d in steps[1:]:
        for copy in far[-d]:
            copy.wait_recv()
    for copy in sg_x + ends:
        copy.wait_recv()
    assert copies.count == N_GATHER, copies.count
    copies.finish()


def attend_kernel(
    kv_ref, qd_ref, st_ref, sg_ref, dkv_ref, dq_ref,
    rows_ref, dq_acc, dk_acc, dv_acc, keys_t, p_ref, ds_ref,
    low_ref, k_list, t_list, from_list,
):
    z, y, x, c = place()
    key_start = y // 2 * 2048 + c * 1024 + y % 2 * 512
    query_start = x * TOK + z * PIECE

    ids = lax.broadcasted_iota(jnp.int32, (IDS, TOK), 0).astype(F32)
    before = jnp.zeros((IDS, TOK), F32)
    for b in range(NZ * NX):
        before += jnp.where(sg_ref[b] < ids, 1.0, 0.0)
    before = jnp.sum(before, axis=1, keepdims=True)
    id_col = lax.broadcasted_iota(jnp.int32, (IDS, QT), 0).astype(F32)
    lane = lax.broadcasted_iota(jnp.int32, (1, 128), 1)
    lane_q = lax.broadcasted_iota(jnp.int32, (1, QT), 1)
    half = lane < ROWS

    for t in range(NQT):
        g = t * TILE_G
        stats = [st_ref[g + i, 0:1, :] for i in range(TILE_G)]
        turned = [pltpu.roll(s, ROWS, 1) for s in stats]
        lse = jnp.concatenate(
            [jnp.where(half, stats[0], turned[1]), jnp.where(half, stats[2], turned[3])], axis=1
        )
        dot = jnp.concatenate(
            [jnp.where(half, turned[0], stats[1]), jnp.where(half, turned[2], stats[3])], axis=1
        )
        seg = [st_ref[g + i, 1:2, :] for i in range(TILE_G)]
        seg = jnp.concatenate(
            [jnp.where(half, seg[0], seg[1]), jnp.where(half, seg[2], seg[3])], axis=1
        )
        lo = jnp.sum(jnp.where(id_col == seg, before, 0.0), axis=0, keepdims=True)
        piece = g + lane_q // ROWS
        rem = piece % NZ * CHUNK + query_start + lane_q % PIECE - key_start
        hi = piece // NZ * CHUNK + jnp.clip(rem + 1, 0, CHUNK)
        rows_ref[t, 0:1, :] = lse * LOG2E
        rows_ref[t, 1:2, :] = dot
        rows_ref[t, 2:3, :] = lo
        rows_ref[t, 3:4, :] = hi.astype(F32)
        low_ref[t] = jnp.min(lo).astype(jnp.int32)

    def clear(k, carry):
        dq_acc[2 * k] = jnp.zeros((HD, QT), F32)
        dq_acc[2 * k + 1] = jnp.zeros((HD, QT), F32)
        dk_acc[k] = jnp.zeros((KT, HD), F32)
        dv_acc[k] = jnp.zeros((KT, HD), F32)
        keys_t[k] = kv_ref[k, :, 0:HD].T
        return carry

    lax.fori_loop(0, NKT, clear, 0)
    p_ref[...] = jnp.zeros((KT, QT), BF)
    ds_ref[...] = jnp.zeros((KT, QT), BF)

    def nothing(n):
        k_list[n] = 0
        t_list[n] = 0
        from_list[n] = -(1 << 20)

    nothing(0)

    def listed(k, count):
        ahead = k * (NZ * CHUNK) + key_start - query_start - (PIECE - 1)
        for t in range(NQT):
            k_list[count] = k
            t_list[count] = t
            from_list[count] = k * KT
            seen = (low_ref[t] < (k + 1) * KT) & (ahead <= (t * TILE_G + TILE_G - 1) * CHUNK)
            count += jnp.where(seen, 1, 0)
        return count

    count = lax.fori_loop(0, NKT, listed, 1)
    nothing(count)

    def step(n, carry):
        k, t = k_list[n], t_list[n]
        q = qd_ref[pl.ds(t * TILE_G, TILE_G), 0].reshape(QT, HD)
        do = qd_ref[pl.ds(t * TILE_G, TILE_G), 1].reshape(QT, HD)
        p, ds = p_ref[...], ds_ref[...]
        dv_acc[k] += jnp.dot(p, do, preferred_element_type=F32)
        dk_acc[k] += jnp.dot(ds, q, preferred_element_type=F32)
        dq_acc[t] += jnp.dot(keys_t[k], ds, preferred_element_type=F32)
        k, t = k_list[n + 1], t_list[n + 1]
        q = qd_ref[pl.ds(t * TILE_G, TILE_G), 0].reshape(QT, HD)
        do = qd_ref[pl.ds(t * TILE_G, TILE_G), 1].reshape(QT, HD)
        start = from_list[n + 1].astype(F32)
        low = rows_ref[t, 2:3, :] - start
        high = rows_ref[t, 3:4, :] - start
        across = (((1,), (1,)), ((), ()))
        for i in range(KT // SUB):
            part = pl.ds(i * SUB, SUB)
            s = lax.dot_general(kv_ref[k, part, 0:HD], q, across, preferred_element_type=F32)
            dp = lax.dot_general(
                kv_ref[k, part, HD:2 * HD], do, across, preferred_element_type=F32
            )
            index = (lax.broadcasted_iota(jnp.int32, (SUB, QT), 0) + i * SUB).astype(F32)
            seen = (index >= low) & (index < high)
            p = jnp.where(seen, jnp.exp2(s * (SCALE * LOG2E) - rows_ref[t, 0:1, :]), 0.0)
            p_ref[part, :] = p.astype(BF)
            ds_ref[part, :] = (p * (dp - rows_ref[t, 1:2, :])).astype(BF)
        return carry

    lax.fori_loop(0, count, step, 0)

    def emit(k, carry):
        dkv_ref[k, :, 0:HD] = (dk_acc[k] * SCALE).astype(BF)
        dkv_ref[k, :, HD:2 * HD] = dv_acc[k].astype(BF)
        for i in range(NQT // NKT):
            t = k * (NQT // NKT) + i
            dq = (dq_acc[t] * SCALE).T
            dq_ref[pl.ds(t * TILE_G, TILE_G)] = dq.astype(BF).reshape(TILE_G, ROWS, HD)
        return carry

    lax.fori_loop(0, NKT, emit, 0)


N_REDUCE = 16 + 16 + 7 + 7 + 4 + 1 + 2 + 2 + 7


def reduce_kernel(
    kv_ref, dq_in, gq_ref, gk_ref, gv_ref,
    far, near, out_x, ring_in, ring_out, both_in, both_out, both_sum, b_far, b_near, b_out,
    q_twin, q_sum, q_far, q_near, q_out, q_send, q_back, send, recv,
):
    z, y, x, c = place()
    xp, xm, xo = (x + 1) % NX, (x + 3) % NX, (x + 2) % NX
    yp, ym, yo = (y + 1) % NY, (y + 3) % NY, (y + 2) % NY
    zp, zm = (z + 1) % NZ, (z + NZ - 1) % NZ
    right, left = device(z, y, xp, c), device(z, y, xm, c)
    up, down = device(z, yp, x, c), device(z, ym, x, c)
    z_right, z_left = device(zp, y, x, c), device(zm, y, x, c)
    twin = device(z, y, x, 1 - c)
    planes = [(z + d) % NZ for d in range(1, NZ)]
    greet([right, left, up, down, twin] + [device(w, y, x, c) for w in planes])
    copies = Copies(send, recv)
    start = copies.start
    h = ROUND // 2
    rest = pl.ds(ROUND, BOTH)
    order = [4, 3, -3, 2, -2, 1, -1, 0]

    def first(n):
        zb = (z + NZ + order[n]) % NZ
        return (
            start(kv_ref.at[zb, xo, pl.ds(0, h)], far.at[n, 0], right),
            start(kv_ref.at[zb, xo, pl.ds(h, h)], far.at[n, 1], left),
        )

    def second(n, pair):
        zb = (z + NZ + order[n]) % NZ
        pair[0].wait_recv()
        out_x[n, 0, 0:h] = (kv_ref[zb, xp, 0:h].astype(F32) + far[n, 0].astype(F32)).astype(BF)
        out_x[n, 0, h:ROUND] = kv_ref[zb, xp, h:ROUND]
        a = start(out_x.at[n, 0], near.at[n, 0], right)
        pair[1].wait_recv()
        out_x[n, 1, 0:h] = kv_ref[zb, xm, 0:h]
        out_x[n, 1, h:ROUND] = (kv_ref[zb, xm, h:ROUND].astype(F32) + far[n, 1].astype(F32)).astype(BF)
        b = start(out_x.at[n, 1], near.at[n, 1], left)
        return a, b

    ring = {}

    def third(n, pair):
        off = order[n]
        zb = (z + NZ + off) % NZ
        pair[0].wait_recv()
        pair[1].wait_recv()
        total = kv_ref[zb, x, 0:ROUND].astype(F32) + near[n, 0].astype(F32) + near[n, 1].astype(F32)
        if off > 0:
            hop = 4 - off
            if hop > 0:
                ring[("r", hop)].wait_recv()
                total += ring_in[hop - 1].astype(F32)
            ring_out[n] = total.astype(BF)
            ring[("r", hop + 1)] = start(ring_out.at[n], ring_in.at[hop], z_right)
        elif off < 0:
            hop = 3 + off
            if hop > 0:
                ring[("l", hop)].wait_recv()
                total += ring_in[4 + hop - 1].astype(F32)
            ring_out[n] = total.astype(BF)
            ring[("l", hop + 1)] = start(ring_out.at[n], ring_in.at[4 + hop], z_left)
        else:
            ring[("r", 4)].wait_recv()
            ring[("l", 3)].wait_recv()
            total += ring_in[3].astype(F32) + ring_in[6].astype(F32)
            gk_ref[0:ROUND] = total[:, 0:HD].astype(BF)
            gv_ref[0:ROUND] = total[:, HD:2 * HD].astype(BF)

    def both(s):
        if s == 0:
            ring["R", 1] = start(kv_ref.at[(z + 4) % NZ, :, rest], both_in.at[0], z_right)
            ring["L", 1] = start(kv_ref.at[(z + 5) % NZ, :, rest], both_in.at[4], z_left)
            return
        if s < 5:
            ring["R", s].wait_recv()
        if s < 4:
            mine = kv_ref[(z + 4 - s) % NZ, :, ROUND:TOK].astype(F32)
            both_out[s - 1] = (mine + both_in[s - 1].astype(F32)).astype(BF)
            ring["R", s + 1] = start(both_out.at[s - 1], both_in.at[s], z_right)
        if s < 3:
            ring["L", s].wait_recv()
            mine = kv_ref[(z + 5 + s) % NZ, :, ROUND:TOK].astype(F32)
            both_out[2 + s] = (mine + both_in[3 + s].astype(F32)).astype(BF)
            ring["L", s + 1] = start(both_out.at[2 + s], both_in.at[4 + s], z_left)
        if s == 4:
            ring["L", 3].wait_recv()
            both_sum[...] = (
                kv_ref[z, :, ROUND:TOK].astype(F32)
                + both_in[3].astype(F32)
                + both_in[6].astype(F32)
            ).astype(BF)
            b = BOTH // 2
            ring["f", 0] = start(both_sum.at[xo, pl.ds(0, b)], b_far.at[0], right)
            ring["f", 1] = start(both_sum.at[xo, pl.ds(b, b)], b_far.at[1], left)
        if s == 5:
            b = BOTH // 2
            ring["f", 0].wait_recv()
            b_out[0, 0:b] = (both_sum[xp, 0:b].astype(F32) + b_far[0].astype(F32)).astype(BF)
            b_out[0, b:BOTH] = both_sum[xp, b:BOTH]
            ring["n", 0] = start(b_out.at[0], b_near.at[0], right)
            ring["f", 1].wait_recv()
            b_out[1, 0:b] = both_sum[xm, 0:b]
            b_out[1, b:BOTH] = (both_sum[xm, b:BOTH].astype(F32) + b_far[1].astype(F32)).astype(BF)
            ring["n", 1] = start(b_out.at[1], b_near.at[1], left)

    def both_end():
        ring["n", 0].wait_recv()
        ring["n", 1].wait_recv()
        total = both_sum[x].astype(F32) + b_near[0].astype(F32) + b_near[1].astype(F32)
        gk_ref[ROUND:TOK] = total[:, 0:HD].astype(BF)
        gv_ref[ROUND:TOK] = total[:, HD:2 * HD].astype(BF)

    swap = start(dq_in.at[:, :, 1 - c], q_twin, twin)
    both(0)
    one = [first(0), first(1)]
    two = []
    for n in range(NZ):
        if n + 2 < NZ:
            one.append(first(n + 2))
        two.append(second(n, one[n]))
        if n == 0:
            swap.wait_recv()
            for zz in range(NZ):
                q_sum[zz] = (dq_in[zz, :, c].astype(F32) + q_twin[zz].astype(F32)).astype(BF)
            q_a = start(q_sum.at[pl.ds(0, 4), yo // 2, yo % 2], q_far.at[0], up)
            q_b = start(q_sum.at[pl.ds(4, 4), yo // 2, yo % 2], q_far.at[1], down)
        if n in (1, 3, 5):
            both(n // 2 + 1)
        if n > 5:
            both(n - 2)
        if n > 0:
            third(n - 1, two[n - 1])
        if n == 2:
            q_a.wait_recv()
            q_out[0, 0:4] = (
                q_sum[0:4, yp // 2, yp % 2].astype(F32) + q_far[0].astype(F32)
            ).astype(BF)
            q_out[0, 4:8] = q_sum[4:8, yp // 2, yp % 2]
            q_c = start(q_out.at[0], q_near.at[0], up)
            q_b.wait_recv()
            q_out[1, 0:4] = q_sum[0:4, ym // 2, ym % 2]
            q_out[1, 4:8] = (
                q_sum[4:8, ym // 2, ym % 2].astype(F32) + q_far[1].astype(F32)
            ).astype(BF)
            q_d = start(q_out.at[1], q_near.at[1], down)
        if n == 5:
            q_c.wait_recv()
            q_d.wait_recv()
            q_send[...] = (
                q_sum[:, y // 2, y % 2].astype(F32)
                + q_near[0].astype(F32)
                + q_near[1].astype(F32)
            ).astype(BF)
            back = [start(q_send.at[w], q_back.at[z], device(w, y, x, c)) for w in planes]
            q_back[z] = q_send[z]
    third(NZ - 1, two[NZ - 1])
    both_end()
    for copy in back:
        copy.wait_recv()
    for w in range(NZ):
        for head in range(GROUP):
            gq_ref[w * PIECE:(w + 1) * PIECE, head * HD:(head + 1) * HD] = q_back[
                w, head * PIECE:(head + 1) * PIECE
            ]
    assert copies.count == N_REDUCE, copies.count
    copies.finish()


def body(queries, keys, values, outputs, out_grad, log_sum_exp, segment_ids):
    hbm = pl.BlockSpec(memory_space=pltpu.HBM)
    vmem = pl.BlockSpec(memory_space=pltpu.VMEM)

    kv_all, qd_all, st_all, sg_all = pl.pallas_call(
        gather_kernel,
        out_shape=[
            jax.ShapeDtypeStruct((NZ, NX, TOK, 2 * HD), BF),
            jax.ShapeDtypeStruct((NZ, 2, NC, 2, 2, ROWS, HD), BF),
            jax.ShapeDtypeStruct((NZ, 2, NC, 2, 2, 128), F32),
            jax.ShapeDtypeStruct((NZ, NX, 1, TOK), F32),
        ],
        in_specs=[hbm] * 7,
        out_specs=[vmem] * 4,
        scratch_shapes=[
            pltpu.VMEM((TOK, GROUP * HD), BF),
            pltpu.VMEM((TOK, GROUP * HD), BF),
            pltpu.VMEM((TOK, GROUP * HD), BF),
            pltpu.VMEM((GROUP, TOK), F32),
            pltpu.VMEM((1, TOK), jnp.int32),
            pltpu.VMEM((NZ, 2, ROWS, HD), BF),
            pltpu.VMEM((NZ, 2, 2 * ROWS), F32),
            pltpu.SemaphoreType.DMA((N_GATHER,)),
            pltpu.SemaphoreType.DMA((N_GATHER,)),
            pltpu.SemaphoreType.DMA((7,)),
        ],
        compiler_params=pltpu.CompilerParams(
            collective_id=0, has_side_effects=True, vmem_limit_bytes=40 * 2**20
        ),
        name="gather",
    )(
        *[
            pltpu.with_memory_space_constraint(a, pltpu.HBM)
            for a in (
                queries, keys, values, outputs, out_grad,
                log_sum_exp.T, segment_ids.reshape(1, TOK),
            )
        ]
    )

    dkv, dq = pl.pallas_call(
        attend_kernel,
        out_shape=[
            jax.ShapeDtypeStruct((NKT, KT, 2 * HD), BF),
            jax.ShapeDtypeStruct((NG, ROWS, HD), BF),
        ],
        in_specs=[vmem] * 4,
        out_specs=[vmem] * 2,
        scratch_shapes=[
            pltpu.VMEM((NQT, 8, QT), F32),
            pltpu.VMEM((NQT, HD, QT), F32),
            pltpu.VMEM((NKT, KT, HD), F32),
            pltpu.VMEM((NKT, KT, HD), F32),
            pltpu.VMEM((NKT, HD, KT), BF),
            pltpu.VMEM((KT, QT), BF),
            pltpu.VMEM((KT, QT), BF),
            pltpu.SMEM((NQT,), jnp.int32),
            pltpu.SMEM((STEPS,), jnp.int32),
            pltpu.SMEM((STEPS,), jnp.int32),
            pltpu.SMEM((STEPS,), jnp.int32),
        ],
        compiler_params=pltpu.CompilerParams(vmem_limit_bytes=40 * 2**20),
        name="attend",
    )(
        kv_all.reshape(NKT, KT, 2 * HD),
        qd_all.reshape(NG, 2, ROWS, HD),
        st_all.reshape(NG, 2, 128),
        sg_all.reshape(NZ * NX, 1, TOK),
    )

    return pl.pallas_call(
        reduce_kernel,
        out_shape=[
            jax.ShapeDtypeStruct((TOK, GROUP * HD), BF),
            jax.ShapeDtypeStruct((TOK, HD), BF),
            jax.ShapeDtypeStruct((TOK, HD), BF),
        ],
        in_specs=[vmem] * 2,
        out_specs=[vmem] * 3,
        scratch_shapes=[
            pltpu.VMEM((NZ, 2, ROUND // 2, 2 * HD), BF),
            pltpu.VMEM((NZ, 2, ROUND, 2 * HD), BF),
            pltpu.VMEM((NZ, 2, ROUND, 2 * HD), BF),
            pltpu.VMEM((7, ROUND, 2 * HD), BF),
            pltpu.VMEM((7, ROUND, 2 * HD), BF),
            pltpu.VMEM((7, NX, BOTH, 2 * HD), BF),
            pltpu.VMEM((5, NX, BOTH, 2 * HD), BF),
            pltpu.VMEM((NX, BOTH, 2 * HD), BF),
            pltpu.VMEM((2, BOTH // 2, 2 * HD), BF),
            pltpu.VMEM((2, BOTH, 2 * HD), BF),
            pltpu.VMEM((2, BOTH, 2 * HD), BF),
            pltpu.VMEM((NZ, 2, 2, ROWS, HD), BF),
            pltpu.VMEM((NZ, 2, 2, ROWS, HD), BF),
            pltpu.VMEM((2, 4, ROWS, HD), BF),
            pltpu.VMEM((2, NZ, ROWS, HD), BF),
            pltpu.VMEM((2, NZ, ROWS, HD), BF),
            pltpu.VMEM((NZ, ROWS, HD), BF),
            pltpu.VMEM((NZ, ROWS, HD), BF),
            pltpu.SemaphoreType.DMA((N_REDUCE,)),
            pltpu.SemaphoreType.DMA((N_REDUCE,)),
        ],
        compiler_params=pltpu.CompilerParams(
            collective_id=1, has_side_effects=True, vmem_limit_bytes=40 * 2**20
        ),
        name="reduce",
    )(
        dkv.reshape(NZ, NX, TOK, 2 * HD),
        dq.reshape(NZ, 2, NC, 2, ROWS, HD),
    )


def solution(mesh):
    rows = P(("row", "col"), None)
    return jax.shard_map(
        body,
        mesh=mesh,
        in_specs=(rows, rows, rows, rows, rows, rows, P(("row", "col"))),
        out_specs=(rows, rows, rows),
        check_vma=False,
    )
```

time: 568 us -> 90 us (0.16)
  waiting for transfers between devices: 343 us -> 0 us
  blocking collectives: 114 us -> 0 us
  Pallas kernels: 0 us -> 87.4 us
  other arithmetic: 46.7 us -> 0 us
  local copies, waits for them, and re-layouts: 32 us -> 1.89 us
  between operations: 14.2 us -> 0.66 us
  matrix products: 11.6 us -> 0 us
    reduce_scatter x2 -> x0, waiting for transfers between devices: 216 us -> none  [the longest x1 132 us: body(): kv_mine = lax.psum_scatter(kv_grads, 'row', scatter_dimension=0, tiled=True)]
    all_gather x4 -> x0, waiting for transfers between devices: 124 us -> none  [the longest x1 77 us: body(): lax.all_gather(values, 'row', axis=0, tiled=True)]
    all_gather x4 -> x0, blocking collectives: 114 us -> none  [the longest x1 43.1 us: body(): lax.all_gather(seg_half, 'row', axis=0, tiled=True)]
    pallas_call x0 -> x3, Pallas kernels: none -> 87.4 us  [the longest x1 36.7 us: body(): pl.pallas_call(gather_kernel, out_shape=[jax.ShapeDtypeStruct((NZ, NX, TO...]
    add x17 -> x0, other arithmetic: 25.3 us -> none  [the longest x8 25.2 us: visit(): return (running + grad_query, grad_kv)]
    dynamic_update_slice x16 -> x0, local copies, waits for them, and re-layouts: 16.6 us -> none  [over_blocks(): lax.scan(visit, jnp.zeros((query_count, query_width), jnp.float32), stacked)]
    reduce_or x8 -> x0, other arithmetic: 16.1 us -> none  [block_grads(): return lax.cond(jnp.any(visible), compute, skipped, 0)]
    dot_general x5 -> x0, matrix products: 11.6 us -> none  [the longest x1 4.01 us: compute(): jnp.einsum('qhgd,khd->hgqk', dout_heads, value_heads, preferred_element_t...]
  transfers between devices with their start and end apart: 6 -> 0, of which waited for: 4 -> 0; matrix products, arithmetic and copies ran while one was open for 1% -> 0% of each run, Pallas kernels for 0% -> 0%
where the time goes in v1:
time: 90 us; the launch traced here: 89.9 us
  Pallas kernels  87.4 us (97%)
  local copies, waits for them, and re-layouts  1.89 us (2%)
    pallas_call x1, Pallas kernels, body(): pl.pallas_call(gather_kernel, out_shape=[jax.ShapeDtypeStruct((NZ, NX, TO...  36.7 us
    pallas_call x1, Pallas kernels, body(): pl.pallas_call(reduce_kernel, out_shape=[jax.ShapeDtypeStruct((TOK, GROUP...  32.6 us
    pallas_call x1, Pallas kernels, body(): pl.pallas_call(attend_kernel, out_shape=[jax.ShapeDtypeStruct((NKT, KT, 2...  18.1 us
    unnamed x3, local copies, waits for them, and re-layouts  1.89 us

profile of v1, /device:TPU:2, one launch (start us, length us, event | category | flops | bytes accessed | tf_op | source)
XLA Modules:
  0.0 89.9 jit_solution(3898985700645343573)
XLA Ops:
  0.6 36.7 %gather.1 = (bf16[8,4,128,256]{3,2,1,0:T(8,128)(2,1)S(1)}, bf16[8,2,2,2,2,64,128]{6,5,4,3,2,1,0:T(8,128)(2,1)S(1)}, f32[8,2,2,2,2,128]{5,4,3,2,1,0:T(2,128)S(1)}, f32[8,4,1,128]{3,2,1,0:T(1,128)S(1)}) custom-call(bf16[128,512]{1,0:T(8,128)(2,1)} %q_in.1, bf16[128,128]{1,0:T(8,128)(2,1)} %k_in.1, bf16[128,128]{1,0:T(8,128)(2,1)} %v_in.1, ...), custom_call_target="tpu_custom_call" | custom-call | tf_op jit(solution)/shard_map/gather/pallas_call | solution.py:595
  37.3 18.1 %attend.1 = (bf16[8,512,256]{2,1,0:T(8,128)(2,1)S(1)}, bf16[64,64,128]{2,1,0:T(8,128)(2,1)S(1)}) custom-call(bf16[8,512,256]{2,1,0:T(8,128)(2,1)S(1)} %bitcast.9, bf16[64,2,64,128]{3,2,1,0:T(8,128)(2,1)S(1)} %bitcast.10, f32[64,2,128]{2,1,0:T(2,128)S(1)} %bitcast.12, f32[32,1,128]{2,1,0:T(1,128)S(1)} %bitcast.13), custom_call_target="tpu_custom_call" | custom-call | tf_op jit(solution)/shard_map/attend/pallas_call | solution.py:631
  55.4 32.6 %reduce.1 = (bf16[128,512]{1,0:T(8,128)(2,1)S(1)}, bf16[128,128]{1,0:T(8,128)(2,1)S(1)}, bf16[128,128]{1,0:T(8,128)(2,1)S(1)}) custom-call(bf16[8,4,128,256]{3,2,1,0:T(8,128)(2,1)S(1)} %bitcast.8, bf16[8,2,2,2,64,128]{5,4,3,2,1,0:T(8,128)(2,1)S(1)} %bitcast.11), custom_call_target="tpu_custom_call" | custom-call | tf_op jit(solution)/shard_map/reduce/pallas_call | solution.py:661
  88.0 0.7 copy.13
  88.7 0.6 copy.14
  89.3 0.6 copy.15

commit v2 on v1

--- a/solution.py
+++ b/solution.py
@@ -77,7 +77,7 @@
     pl.semaphore_wait(barrier, len(peers))
 
 
-N_GATHER = 32 + 7 + 7 + 7 + 24 + 4 + 11 + 10
+N_GATHER = 32 + 7 + 7 + 24 + 4 + 11 + 10
 
 
 def gather_kernel(
@@ -114,45 +114,46 @@
     start = copies.start
     yh, yl = y // 2, y % 2
 
-    def spread(d):
-        zb = (z + NZ + d) % NZ
-        count = TOK if d == 0 else ROUND
-        src = kv_all.at[zb, x, pl.ds(0, count)]
-        near[d] = (start(src, src, right), start(src, src, left))
-
-    def pass_on(d):
-        zb = (z + NZ + d) % NZ
-        count = (TOK if d == 0 else ROUND) // 2
-        near[d][0].wait_recv()
-        src = kv_all.at[zb, xm, pl.ds(0, count)]
-        far[d] = [start(src, src, right)]
-        near[d][1].wait_recv()
-        src = kv_all.at[zb, xp, pl.ds(count, count)]
-        far[d].append(start(src, src, left))
-
-    def ring_a(s):
+    near, far, hops, pieces, q_near, q_far = {}, {}, {}, {}, {}, []
+    few, ends = {}, []
+    steps = [0, 1, -1, 2, -2, 3, -3, 4]
+    h = TOK // 2
+
+    def ring(s):
         if s > 0:
             hops["r", s].wait_recv()
         if s < 4:
-            src = kv_all.at[(z + NZ - s) % NZ, x, pl.ds(0, ROUND)]
+            src = kv_all.at[(z + NZ - s) % NZ, x]
             hops["r", s + 1] = start(src, src, z_right)
         if 0 < s < 4:
             hops["l", s].wait_recv()
         if s < 3:
-            src = kv_all.at[(z + s) % NZ, x, pl.ds(0, ROUND)]
+            src = kv_all.at[(z + s) % NZ, x]
             hops["l", s + 1] = start(src, src, z_left)
 
-    def ring_b(s):
-        if s > 0:
-            hops["R", s].wait_recv()
-        if s < 4:
-            src = kv_all.at[(z + NZ - s) % NZ, :, pl.ds(ROUND, BOTH)]
-            hops["R", s + 1] = start(src, src, z_right)
-        if 0 < s < 4:
-            hops["L", s].wait_recv()
-        if s < 3:
-            src = kv_all.at[(z + s) % NZ, :, pl.ds(ROUND, BOTH)]
-            hops["L", s + 1] = start(src, src, z_left)
+    def spread(d):
+        src = kv_all.at[(z + NZ + d) % NZ, x]
+        near[d] = (start(src, src, right), start(src, src, left))
+
+    def pass_on(d):
+        zb = (z + NZ + d) % NZ
+        near[d][0].wait_recv()
+        src = kv_all.at[zb, xm, pl.ds(0, h)]
+        far[d] = [start(src, src, right)]
+        near[d][1].wait_recv()
+        src = kv_all.at[zb, xp, pl.ds(h, h)]
+        far[d].append(start(src, src, left))
+
+    def pack(_):
+        load[2].wait()
+        load[3].wait()
+        for w in range(NZ):
+            for g in range(GROUP):
+                here = (slice(w * PIECE, (w + 1) * PIECE), slice(g * HD, (g + 1) * HD))
+                there = slice(g * PIECE, (g + 1) * PIECE)
+                qd_ref[w, 0, there] = q_ref[here]
+                qd_ref[w, 1, there] = do_ref[here]
+        qd_all[z, yh, c, yl] = qd_ref[z]
 
     def q_send(d):
         w = (z + NZ + d) % NZ
@@ -175,125 +176,81 @@
             src = qd_all.at[zz, yp // 2, c, yp % 2]
             q_far.append(start(src, src, down))
 
-    def q_across(yy):
-        src = qd_all.at[:, yy // 2, c, yy % 2]
-        ends.append(start(src, src, twin))
-
-    near, far, hops, pieces, q_near, q_far, ends = {}, {}, {}, {}, {}, [], []
-    steps = [0, 1, -1, 2, -2, 3, -3, 4]
+    def q_across(where):
+        if where == 2:
+            for copy in q_far:
+                copy.wait_recv()
+        for yy in ((y,), (yp, ym), (yo,))[where]:
+            src = qd_all.at[:, yy // 2, c, yy % 2]
+            ends.append(start(src, src, twin))
+
+    def stats(stage):
+        if stage == 0:
+            for copy in load[4:]:
+                copy.wait()
+            sub = lax.broadcasted_iota(jnp.int32, (TOK, TOK), 0)
+            lane = lax.broadcasted_iota(jnp.int32, (TOK, TOK), 1)
+            dots = []
+            for g in range(GROUP):
+                cols = slice(g * HD, (g + 1) * HD)
+                both = lax.dot_general(
+                    do_ref[:, cols], o_ref[:, cols], (((1,), (1,)), ((), ())),
+                    preferred_element_type=F32,
+                )
+                dots.append(jnp.sum(jnp.where(sub == lane, both, 0.0), axis=0, keepdims=True))
+            numbers = jnp.concatenate([lse_ref[...]] + dots, axis=0)
+            seg = seg_ref[...].astype(F32)
+            sg_all[z, x] = seg
+            segs = jnp.broadcast_to(seg, (2 * GROUP, TOK))
+            sub, block = sub[0:8], lane[0:8] // PIECE
+            turned = [
+                [a if d == 0 else pltpu.roll(a, d * PIECE, 1) for d in range(NZ)]
+                for a in (numbers, segs)
+            ]
+            for w in range(NZ):
+                for i in range(2):
+                    row = jnp.zeros((8, TOK), F32)
+                    for d in range(NZ):
+                        fits = (block == sub) & ((sub + NZ - w) % NZ == d)
+                        row += jnp.where(fits, turned[i][d], 0.0)
+                    st_ref[w, i:i + 1, :] = jnp.sum(row, axis=0, keepdims=True)
+            st_all[z, yh, c, yl] = st_ref[z]
+            few[0] = [
+                start(st_ref.at[w], st_all.at[z, yh, c, yl], device(w, y, x, c)) for w in planes
+            ]
+            src = sg_all.at[z, x]
+            few[0] += [start(src, src, device(w, y, x, c)) for w in planes]
+        elif stage == 1:
+            for copy in few[0]:
+                copy.wait_recv()
+            src = st_all.at[:, yh, c, yl]
+            few[1] = [start(src, src, to) for to in (up, down, beyond)]
+            src = sg_all.at[:, x]
+            ends.extend([start(src, src, to) for to in (right, left, across)])
+        else:
+            for copy in few[1]:
+                copy.wait_recv()
+            src = st_all.at[:, :, c]
+            ends.append(start(src, src, twin))
+
     load[0].wait()
     load[1].wait()
-    spread(0)
-    ring_a(0)
-    load[2].wait()
-    load[3].wait()
-    for w in range(NZ):
-        for h in range(GROUP):
-            here = (slice(w * PIECE, (w + 1) * PIECE), slice(h * HD, (h + 1) * HD))
-            there = slice(h * PIECE, (h + 1) * PIECE)
-            qd_ref[w, 0, there] = q_ref[here]
-            qd_ref[w, 1, there] = do_ref[here]
-    for d in (1, -1, 2, -2):
-        q_send(d)
-    qd_all[z, yh, c, yl] = qd_ref[z]
-    q_share(0)
-
-    for copy in load[4:]:
-        copy.wait()
-    sub = lax.broadcasted_iota(jnp.int32, (TOK, TOK), 0)
-    lane = lax.broadcasted_iota(jnp.int32, (TOK, TOK), 1)
-    dots = []
-    for h in range(GROUP):
-        cols = slice(h * HD, (h + 1) * HD)
-        both = lax.dot_general(
-            do_ref[:, cols], o_ref[:, cols], (((1,), (1,)), ((), ())),
-            preferred_element_type=F32,
-        )
-        dots.append(jnp.sum(jnp.where(sub == lane, both, 0.0), axis=0, keepdims=True))
-    stats = jnp.concatenate([lse_ref[...]] + dots, axis=0)
-    seg = seg_ref[...].astype(F32)
-    sg_all[z, x] = seg
-    segs = jnp.broadcast_to(seg, (2 * GROUP, TOK))
-    sub, block = sub[0:8], lane[0:8] // PIECE
-    turned = [
-        [a if d == 0 else pltpu.roll(a, d * PIECE, 1) for d in range(NZ)] for a in (stats, segs)
-    ]
-    for w in range(NZ):
-        for i in range(2):
-            row = jnp.zeros((8, TOK), F32)
-            for d in range(NZ):
-                row += jnp.where((block == sub) & ((sub + NZ - w) % NZ == d), turned[i][d], 0.0)
-            st_ref[w, i:i + 1, :] = jnp.sum(row, axis=0, keepdims=True)
-    small = [
-        start(st_ref.at[w], st_all.at[z, yh, c, yl], device(w, y, x, c)) for w in planes
-    ]
-    sg_ref = sg_all.at[z, x]
-    marks = [start(sg_ref, sg_ref, device(w, y, x, c)) for w in planes]
-    st_all[z, yh, c, yl] = st_ref[z]
-
-    ring_a(1)
-    spread(-1)
-    spread(1)
-    pass_on(0)
-    ring_a(2)
-    spread(-2)
-    spread(2)
-    for d in (3, -3, 4):
-        q_send(d)
-    for copy in far[0]:
-        copy.wait_recv()
-    ring_b(0)
-    q_share(1)
-    q_share(-1)
-    pass_on(-1)
-    ring_a(3)
-    spread(-3)
-    spread(3)
-    pass_on(1)
-    q_share(2)
-    q_share(-2)
-    q_pass(0)
-    q_pass(1)
-    ring_b(1)
-    pass_on(-2)
-    ring_a(4)
-    spread(-4)
-    q_pass(-1)
-    for copy in small + marks:
-        copy.wait_recv()
-    few = st_all.at[:, yh, c, yl]
-    st_y = [start(few, few, to) for to in (up, down, beyond)]
-    few = sg_all.at[:, x]
-    sg_x = [start(few, few, to) for to in (right, left, across)]
-    pass_on(2)
-    q_share(3)
-    q_share(-3)
-    q_share(4)
-    q_across(y)
-    ring_b(2)
-    q_pass(2)
-    q_pass(-2)
-    pass_on(-3)
-    for copy in st_y:
-        copy.wait_recv()
-    few = st_all.at[:, :, c]
-    ends.append(start(few, few, twin))
-    pass_on(3)
-    ring_b(3)
-    q_pass(3)
-    q_pass(-3)
-    q_pass(4)
-    q_across(yp)
-    q_across(ym)
-    pass_on(-4)
-    for copy in q_far:
-        copy.wait_recv()
-    q_across(yo)
-    ring_b(4)
-    for d in steps[1:]:
-        for copy in far[-d]:
+    for do, which in [
+        (spread, 0), (ring, 0), (pack, 0), (q_send, 2), (q_send, 1), (q_send, -3), (ring, 1),
+        (spread, -1), (spread, 1), (q_send, 4), (q_send, -1), (q_send, -2), (stats, 0),
+        (pass_on, -1), (ring, 2), (q_share, 1), (spread, 2), (spread, -2), (q_share, 0),
+        (pass_on, 1), (q_share, -3), (q_send, 3), (q_share, -2), (q_share, 2), (pass_on, 2),
+        (q_share, 4), (q_share, -1), (ring, 3), (q_pass, -3), (spread, 3), (q_pass, 2),
+        (spread, -3), (stats, 1), (q_share, 3), (q_pass, 4), (q_pass, -2), (pass_on, -2),
+        (q_pass, 0), (ring, 4), (spread, -4), (q_pass, 1), (q_across, 0), (q_pass, -1),
+        (q_pass, 3), (q_across, 1), (pass_on, 3), (pass_on, 0), (stats, 2), (pass_on, -3),
+        (pass_on, -4), (q_across, 2),
+    ]:
+        do(which)
+    for d in far:
+        for copy in far[d]:
             copy.wait_recv()
-    for copy in sg_x + ends:
+    for copy in ends:
         copy.wait_recv()
     assert copies.count == N_GATHER, copies.count
     copies.finish()
@@ -302,7 +259,7 @@
 def attend_kernel(
     kv_ref, qd_ref, st_ref, sg_ref, dkv_ref, dq_ref,
     rows_ref, dq_acc, dk_acc, dv_acc, keys_t, p_ref, ds_ref,
-    low_ref, k_list, t_list, from_list,
+    low_ref, high_ref, k_list, t_list, from_list, full_list,
 ):
     z, y, x, c = place()
     key_start = y // 2 * 2048 + c * 1024 + y % 2 * 512
@@ -341,6 +298,7 @@
         rows_ref[t, 2:3, :] = lo
         rows_ref[t, 3:4, :] = hi.astype(F32)
         low_ref[t] = jnp.min(lo).astype(jnp.int32)
+        high_ref[t] = jnp.max(lo).astype(jnp.int32)
 
     def clear(k, carry):
         dq_acc[2 * k] = jnp.zeros((HD, QT), F32)
@@ -358,6 +316,7 @@
         k_list[n] = 0
         t_list[n] = 0
         from_list[n] = -(1 << 20)
+        full_list[n] = 0
 
     nothing(0)
 
@@ -367,6 +326,10 @@
             k_list[count] = k
             t_list[count] = t
             from_list[count] = k * KT
+            whole = (high_ref[t] <= k * KT) & (
+                k * (NZ * CHUNK) + key_start + KT - 1 <= t * TILE_G * CHUNK + query_start
+            )
+            full_list[count] = jnp.where(whole, 1, 0)
             seen = (low_ref[t] < (k + 1) * KT) & (ahead <= (t * TILE_G + TILE_G - 1) * CHUNK)
             count += jnp.where(seen, 1, 0)
         return count
@@ -374,7 +337,7 @@
     count = lax.fori_loop(0, NKT, listed, 1)
     nothing(count)
 
-    def step(n, carry):
+    def work(n, masked):
         k, t = k_list[n], t_list[n]
         q = qd_ref[pl.ds(t * TILE_G, TILE_G), 0].reshape(QT, HD)
         do = qd_ref[pl.ds(t * TILE_G, TILE_G), 1].reshape(QT, HD)
@@ -395,11 +358,24 @@
             dp = lax.dot_general(
                 kv_ref[k, part, HD:2 * HD], do, across, preferred_element_type=F32
             )
-            index = (lax.broadcasted_iota(jnp.int32, (SUB, QT), 0) + i * SUB).astype(F32)
-            seen = (index >= low) & (index < high)
-            p = jnp.where(seen, jnp.exp2(s * (SCALE * LOG2E) - rows_ref[t, 0:1, :]), 0.0)
+            p = jnp.exp2(s * (SCALE * LOG2E) - rows_ref[t, 0:1, :])
+            if masked:
+                index = (lax.broadcasted_iota(jnp.int32, (SUB, QT), 0) + i * SUB).astype(F32)
+                p = jnp.where((index >= low) & (index < high), p, 0.0)
             p_ref[part, :] = p.astype(BF)
             ds_ref[part, :] = (p * (dp - rows_ref[t, 1:2, :])).astype(BF)
+
+    def step(n, carry):
+        whole = full_list[n + 1] == 1
+
+        @pl.when(whole)
+        def _():
+            work(n, False)
+
+        @pl.when(jnp.logical_not(whole))
+        def _():
+            work(n, True)
+
         return carry
 
     lax.fori_loop(0, count, step, 0)
@@ -490,25 +466,25 @@
 
     def both(s):
         if s == 0:
-            ring["R", 1] = start(kv_ref.at[(z + 4) % NZ, :, rest], both_in.at[0], z_right)
-            ring["L", 1] = start(kv_ref.at[(z + 5) % NZ, :, rest], both_in.at[4], z_left)
+            ring["R", 1] = start(kv_ref.at[(z + 3) % NZ, :, rest], both_in.at[0], z_right)
+            ring["L", 1] = start(kv_ref.at[(z + 4) % NZ, :, rest], both_in.at[3], z_left)
             return
-        if s < 5:
+        if s < 4:
             ring["R", s].wait_recv()
-        if s < 4:
-            mine = kv_ref[(z + 4 - s) % NZ, :, ROUND:TOK].astype(F32)
+        if s < 3:
+            mine = kv_ref[(z + 3 - s) % NZ, :, ROUND:TOK].astype(F32)
             both_out[s - 1] = (mine + both_in[s - 1].astype(F32)).astype(BF)
             ring["R", s + 1] = start(both_out.at[s - 1], both_in.at[s], z_right)
-        if s < 3:
+        if s < 5:
             ring["L", s].wait_recv()
-            mine = kv_ref[(z + 5 + s) % NZ, :, ROUND:TOK].astype(F32)
-            both_out[2 + s] = (mine + both_in[3 + s].astype(F32)).astype(BF)
-            ring["L", s + 1] = start(both_out.at[2 + s], both_in.at[4 + s], z_left)
+        if s < 4:
+            mine = kv_ref[(z + 4 + s) % NZ, :, ROUND:TOK].astype(F32)
+            both_out[1 + s] = (mine + both_in[2 + s].astype(F32)).astype(BF)
+            ring["L", s + 1] = start(both_out.at[1 + s], both_in.at[3 + s], z_left)
         if s == 4:
-            ring["L", 3].wait_recv()
             both_sum[...] = (
                 kv_ref[z, :, ROUND:TOK].astype(F32)
-                + both_in[3].astype(F32)
+                + both_in[2].astype(F32)
                 + both_in[6].astype(F32)
             ).astype(BF)
             b = BOTH // 2
@@ -532,52 +508,64 @@
         gk_ref[ROUND:TOK] = total[:, 0:HD].astype(BF)
         gv_ref[ROUND:TOK] = total[:, HD:2 * HD].astype(BF)
 
-    swap = start(dq_in.at[:, :, 1 - c], q_twin, twin)
-    both(0)
-    one = [first(0), first(1)]
-    two = []
-    for n in range(NZ):
-        if n + 2 < NZ:
-            one.append(first(n + 2))
-        two.append(second(n, one[n]))
-        if n == 0:
-            swap.wait_recv()
+    queue = {}
+
+    def q_step(s):
+        if s == 0:
+            queue["twin"] = start(dq_in.at[:, :, 1 - c], q_twin, twin)
+        elif s == 1:
+            queue["twin"].wait_recv()
             for zz in range(NZ):
                 q_sum[zz] = (dq_in[zz, :, c].astype(F32) + q_twin[zz].astype(F32)).astype(BF)
-            q_a = start(q_sum.at[pl.ds(0, 4), yo // 2, yo % 2], q_far.at[0], up)
-            q_b = start(q_sum.at[pl.ds(4, 4), yo // 2, yo % 2], q_far.at[1], down)
-        if n in (1, 3, 5):
-            both(n // 2 + 1)
-        if n > 5:
-            both(n - 2)
-        if n > 0:
-            third(n - 1, two[n - 1])
-        if n == 2:
-            q_a.wait_recv()
+            queue["a"] = start(q_sum.at[pl.ds(0, 4), yo // 2, yo % 2], q_far.at[0], up)
+            queue["b"] = start(q_sum.at[pl.ds(4, 4), yo // 2, yo % 2], q_far.at[1], down)
+        elif s == 2:
+            queue["a"].wait_recv()
             q_out[0, 0:4] = (
                 q_sum[0:4, yp // 2, yp % 2].astype(F32) + q_far[0].astype(F32)
             ).astype(BF)
             q_out[0, 4:8] = q_sum[4:8, yp // 2, yp % 2]
-            q_c = start(q_out.at[0], q_near.at[0], up)
-            q_b.wait_recv()
+            queue["c"] = start(q_out.at[0], q_near.at[0], up)
+            queue["b"].wait_recv()
             q_out[1, 0:4] = q_sum[0:4, ym // 2, ym % 2]
             q_out[1, 4:8] = (
                 q_sum[4:8, ym // 2, ym % 2].astype(F32) + q_far[1].astype(F32)
             ).astype(BF)
-            q_d = start(q_out.at[1], q_near.at[1], down)
-        if n == 5:
-            q_c.wait_recv()
-            q_d.wait_recv()
+            queue["d"] = start(q_out.at[1], q_near.at[1], down)
+        else:
+            queue["c"].wait_recv()
+            queue["d"].wait_recv()
             q_send[...] = (
                 q_sum[:, y // 2, y % 2].astype(F32)
                 + q_near[0].astype(F32)
                 + q_near[1].astype(F32)
             ).astype(BF)
-            back = [start(q_send.at[w], q_back.at[z], device(w, y, x, c)) for w in planes]
+            queue["back"] = [
+                start(q_send.at[w], q_back.at[z], device(w, y, x, c)) for w in planes
+            ]
             q_back[z] = q_send[z]
-    third(NZ - 1, two[NZ - 1])
+
+    one, two = {}, {}
+
+    def x_far(n):
+        one[n] = first(n)
+
+    def x_near(n):
+        two[n] = second(n, one[n])
+
+    def x_sum(n):
+        third(n, two[n])
+
+    for do, which in [
+        (q_step, 0), (x_far, 0), (both, 0), (x_far, 1), (x_far, 2), (x_far, 3), (x_near, 0),
+        (x_far, 4), (x_near, 1), (x_far, 5), (both, 1), (q_step, 1), (x_sum, 0), (x_near, 2),
+        (x_far, 6), (x_near, 3), (both, 2), (q_step, 2), (x_sum, 1), (x_near, 4), (x_far, 7),
+        (x_sum, 2), (x_near, 5), (both, 3), (x_near, 6), (x_sum, 3), (x_sum, 4), (q_step, 3),
+        (both, 4), (x_near, 7), (x_sum, 5), (x_sum, 6), (both, 5), (x_sum, 7),
+    ]:
+        do(which)
     both_end()
-    for copy in back:
+    for copy in queue["back"]:
         copy.wait_recv()
     for w in range(NZ):
         for head in range(GROUP):
@@ -645,6 +633,8 @@
             pltpu.VMEM((KT, QT), BF),
             pltpu.VMEM((KT, QT), BF),
             pltpu.SMEM((NQT,), jnp.int32),
+            pltpu.SMEM((NQT,), jnp.int32),
+            pltpu.SMEM((STEPS,), jnp.int32),
             pltpu.SMEM((STEPS,), jnp.int32),
             pltpu.SMEM((STEPS,), jnp.int32),
             pltpu.SMEM((STEPS,), jnp.int32),

time: 90 us -> 83.7 us (0.930)
  Pallas kernels: 87.4 us -> 80.8 us
    pallas_call x1, Pallas kernels: 32.6 us -> 27.2 us  [body(): pl.pallas_call(reduce_kernel, out_shape=[jax.ShapeDtypeStruct((TOK, GROUP...]
    pallas_call x1, Pallas kernels: 36.7 us -> 35.1 us  [body(): pl.pallas_call(gather_kernel, out_shape=[jax.ShapeDtypeStruct((NZ, NX, TO...]
where the time goes in v2:
time: 83.7 us; the launch traced here: 83.3 us
  Pallas kernels  80.8 us (97%)
  local copies, waits for them, and re-layouts  1.89 us (2%)
    pallas_call x1, Pallas kernels, body(): pl.pallas_call(gather_kernel, out_shape=[jax.ShapeDtypeStruct((NZ, NX, TO...  35.1 us
    pallas_call x1, Pallas kernels, body(): pl.pallas_call(reduce_kernel, out_shape=[jax.ShapeDtypeStruct((TOK, GROUP...  27.2 us
    pallas_call x1, Pallas kernels, body(): pl.pallas_call(attend_kernel, out_shape=[jax.ShapeDtypeStruct((NKT, KT, 2...  18.4 us
    unnamed x3, local copies, waits for them, and re-layouts  1.89 us

profile of v2, /device:TPU:2, one launch (start us, length us, event | category | flops | bytes accessed | tf_op | source)
XLA Modules:
  0.0 83.3 jit_solution(7093620305775965220)
XLA Ops:
  0.6 35.1 %gather.1 = (bf16[8,4,128,256]{3,2,1,0:T(8,128)(2,1)S(1)}, bf16[8,2,2,2,2,64,128]{6,5,4,3,2,1,0:T(8,128)(2,1)S(1)}, f32[8,2,2,2,2,128]{5,4,3,2,1,0:T(2,128)S(1)}, f32[8,4,1,128]{3,2,1,0:T(1,128)S(1)}) custom-call(bf16[128,512]{1,0:T(8,128)(2,1)} %q_in.1, bf16[128,128]{1,0:T(8,128)(2,1)} %k_in.1, bf16[128,128]{1,0:T(8,128)(2,1)} %v_in.1, ...), custom_call_target="tpu_custom_call" | custom-call | tf_op jit(solution)/shard_map/gather/pallas_call | solution.py:583
  35.8 18.4 %attend.1 = (bf16[8,512,256]{2,1,0:T(8,128)(2,1)S(1)}, bf16[64,64,128]{2,1,0:T(8,128)(2,1)S(1)}) custom-call(bf16[8,512,256]{2,1,0:T(8,128)(2,1)S(1)} %bitcast.9, bf16[64,2,64,128]{3,2,1,0:T(8,128)(2,1)S(1)} %bitcast.10, f32[64,2,128]{2,1,0:T(2,128)S(1)} %bitcast.12, f32[32,1,128]{2,1,0:T(1,128)S(1)} %bitcast.13), custom_call_target="tpu_custom_call" | custom-call | tf_op jit(solution)/shard_map/attend/pallas_call | solution.py:619
  54.2 27.2 %reduce.1 = (bf16[128,512]{1,0:T(8,128)(2,1)S(1)}, bf16[128,128]{1,0:T(8,128)(2,1)S(1)}, bf16[128,128]{1,0:T(8,128)(2,1)S(1)}) custom-call(bf16[8,4,128,256]{3,2,1,0:T(8,128)(2,1)S(1)} %bitcast.8, bf16[8,2,2,2,64,128]{5,4,3,2,1,0:T(8,128)(2,1)S(1)} %bitcast.11), custom_call_target="tpu_custom_call" | custom-call | tf_op jit(solution)/shard_map/reduce/pallas_call | solution.py:651
  81.4 0.7 copy.13
  82.1 0.6 copy.14
  82.7 0.6 copy.15

commit v3 on v2

--- a/solution.py
+++ b/solution.py
@@ -27,7 +27,7 @@
 NKT = NKEY // KT
 CHUNK = NX * TOK
 IDS = 72
-STEPS = NQT * NKT + 4
+STEPS = NQT * NKT + 8
 SCALE = HD ** -0.5
 LOG2E = math.log2(math.e)
 BF = jnp.bfloat16
@@ -44,6 +44,14 @@
 
 def device(z, y, x, c):
     return (z * 4 + y // 2 * 2 + c, y % 2 * 4 + x)
+
+
+def origin(z, y, x, c):
+    return y // 2 * 2048 + c * 1024 + y % 2 * 512, x * TOK + z * PIECE, c * 2 + y % 2
+
+
+def tile_start(t, shift):
+    return jnp.minimum(t * TILE_G + shift, NG - TILE_G)
 
 
 class Copies:
@@ -70,10 +78,12 @@
             copy.wait_send()
 
 
-def greet(peers):
+def greet(peers, meanwhile=None):
     barrier = pltpu.get_barrier_semaphore()
     for peer in peers:
         pl.semaphore_signal(barrier, inc=1, device_id=peer, device_id_type=MESH)
+    if meanwhile is not None:
+        meanwhile()
     pl.semaphore_wait(barrier, len(peers))
 
 
@@ -81,8 +91,8 @@
 
 
 def gather_kernel(
-    q_in, k_in, v_in, o_in, do_in, lse_in, seg_in, kv_all, qd_all, st_all, sg_all,
-    q_ref, o_ref, do_ref, lse_ref, seg_ref, qd_ref, st_ref, send, recv, local,
+    q_in, k_in, v_in, o_in, do_in, lse_in, seg_in, kv_all, qd_all, keys_t, rows_ref,
+    st_all, sg_all, q_ref, o_ref, do_ref, lse_ref, seg_ref, qd_ref, st_ref, send, recv, local,
 ):
     z, y, x, c = place()
     xp, xm, xo = (x + 1) % NX, (x + 3) % NX, (x + 2) % NX
@@ -120,14 +130,14 @@
     h = TOK // 2
 
     def ring(s):
-        if s > 0:
+        if 0 < s < 4:
             hops["r", s].wait_recv()
-        if s < 4:
+        if s < 3:
             src = kv_all.at[(z + NZ - s) % NZ, x]
             hops["r", s + 1] = start(src, src, z_right)
-        if 0 < s < 4:
+        if s > 0:
             hops["l", s].wait_recv()
-        if s < 3:
+        if s < 4:
             src = kv_all.at[(z + s) % NZ, x]
             hops["l", s + 1] = start(src, src, z_left)
 
@@ -226,30 +236,79 @@
             src = st_all.at[:, yh, c, yl]
             few[1] = [start(src, src, to) for to in (up, down, beyond)]
             src = sg_all.at[:, x]
-            ends.extend([start(src, src, to) for to in (right, left, across)])
+            few[2] = [start(src, src, to) for to in (right, left, across)]
         else:
             for copy in few[1]:
                 copy.wait_recv()
             src = st_all.at[:, :, c]
-            ends.append(start(src, src, twin))
+            few[2].append(start(src, src, twin))
+
+    def turn(d):
+        zb = (z + NZ + d) % NZ
+        for copy in far[d]:
+            copy.wait_recv()
+        for i in range(NX):
+            keys_t[zb, :, i * TOK:(i + 1) * TOK] = kv_all[zb, i, :, 0:HD].T
+
+    def ranges(_):
+        for copy in few[2]:
+            copy.wait_recv()
+        key_start, query_start, shift = origin(z, y, x, c)
+        ids = lax.broadcasted_iota(jnp.int32, (IDS, TOK), 0).astype(F32)
+        before = jnp.zeros((IDS, TOK), F32)
+        for zz in range(NZ):
+            for xx in range(NX):
+                before += jnp.where(sg_all[zz, xx] < ids, 1.0, 0.0)
+        before = jnp.sum(before, axis=1, keepdims=True)
+        id_col = lax.broadcasted_iota(jnp.int32, (IDS, QT), 0).astype(F32)
+        half = lax.broadcasted_iota(jnp.int32, (1, 128), 1) < ROWS
+        lane = lax.broadcasted_iota(jnp.int32, (1, QT), 1)
+
+        def one_tile(t, carry):
+            first = t * TILE_G + shift
+            g = tile_start(t, shift)
+
+            def numbers(i, row):
+                p = g + i
+                return st_all[p // 8, p // 4 % 2, p // 2 % 2, p % 2, row:row + 1, :]
+
+            def pair(a, b):
+                return jnp.where(half, a, b)
+
+            own = [numbers(i, 0) for i in range(TILE_G)]
+            over = [pltpu.roll(a, ROWS, 1) for a in own]
+            lse = jnp.concatenate([pair(own[0], over[1]), pair(own[2], over[3])], axis=1)
+            dot = jnp.concatenate([pair(over[0], own[1]), pair(over[2], own[3])], axis=1)
+            seg = [numbers(i, 1) for i in range(TILE_G)]
+            seg = jnp.concatenate([pair(seg[0], seg[1]), pair(seg[2], seg[3])], axis=1)
+            lo = jnp.sum(jnp.where(id_col == seg, before, 0.0), axis=0, keepdims=True)
+            piece = g + lane // ROWS
+            rem = piece % NZ * CHUNK + query_start + lane % PIECE - key_start
+            hi = piece // NZ * CHUNK + jnp.clip(rem + 1, 0, CHUNK)
+            fresh = piece >= first
+            rows_ref[t, 0:1, :] = lse * LOG2E
+            rows_ref[t, 1:2, :] = dot
+            rows_ref[t, 2:3, :] = jnp.where(fresh, lo, float(NKEY))
+            rows_ref[t, 3:4, :] = jnp.where(fresh, hi, 0).astype(F32)
+            return carry
+
+        lax.fori_loop(0, NQT, one_tile, 0)
 
     load[0].wait()
     load[1].wait()
     for do, which in [
-        (spread, 0), (ring, 0), (pack, 0), (q_send, 2), (q_send, 1), (q_send, -3), (ring, 1),
-        (spread, -1), (spread, 1), (q_send, 4), (q_send, -1), (q_send, -2), (stats, 0),
-        (pass_on, -1), (ring, 2), (q_share, 1), (spread, 2), (spread, -2), (q_share, 0),
-        (pass_on, 1), (q_share, -3), (q_send, 3), (q_share, -2), (q_share, 2), (pass_on, 2),
-        (q_share, 4), (q_share, -1), (ring, 3), (q_pass, -3), (spread, 3), (q_pass, 2),
-        (spread, -3), (stats, 1), (q_share, 3), (q_pass, 4), (q_pass, -2), (pass_on, -2),
-        (q_pass, 0), (ring, 4), (spread, -4), (q_pass, 1), (q_across, 0), (q_pass, -1),
-        (q_pass, 3), (q_across, 1), (pass_on, 3), (pass_on, 0), (stats, 2), (pass_on, -3),
-        (pass_on, -4), (q_across, 2),
+        (spread, 0), (ring, 0), (pack, 0), (q_send, -1), (q_share, 0), (q_send, 3), (q_send, -2),
+        (ring, 1), (q_send, -3), (q_send, 1), (spread, 1), (q_send, 4), (pass_on, 0),
+        (spread, -1), (stats, 0), (q_share, 3), (q_share, -1), (ring, 2), (spread, -2),
+        (q_send, 2), (spread, 2), (q_pass, 3), (pass_on, -1), (q_share, -2), (stats, 1),
+        (q_pass, 0), (pass_on, -2), (q_share, 4), (pass_on, 1), (ring, 3), (q_share, 1),
+        (spread, -3), (q_share, -3), (spread, 3), (q_share, 2), (q_pass, -2), (stats, 2),
+        (turn, -2), (turn, -1), (q_pass, 1), (q_pass, 4), (q_across, 0), (q_pass, -1), (ring, 4),
+        (spread, 4), (pass_on, 2), (pass_on, -3), (q_pass, -3), (q_pass, 2), (q_across, 1),
+        (ranges, 0), (turn, 1), (pass_on, 3), (pass_on, 4), (q_across, 2), (turn, 2), (turn, 0),
+        (turn, 3), (turn, -3), (turn, 4),
     ]:
         do(which)
-    for d in far:
-        for copy in far[d]:
-            copy.wait_recv()
     for copy in ends:
         copy.wait_recv()
     assert copies.count == N_GATHER, copies.count
@@ -257,98 +316,69 @@
 
 
 def attend_kernel(
-    kv_ref, qd_ref, st_ref, sg_ref, dkv_ref, dq_ref,
-    rows_ref, dq_acc, dk_acc, dv_acc, keys_t, p_ref, ds_ref,
-    low_ref, high_ref, k_list, t_list, from_list, full_list,
+    kv_ref, qd_ref, keys_t, rows_ref, dq_acc, dk_acc, dv_acc, p_ref, ds_ref,
+    low_ref, k_list, t_list, from_list,
 ):
     z, y, x, c = place()
-    key_start = y // 2 * 2048 + c * 1024 + y % 2 * 512
-    query_start = x * TOK + z * PIECE
-
-    ids = lax.broadcasted_iota(jnp.int32, (IDS, TOK), 0).astype(F32)
-    before = jnp.zeros((IDS, TOK), F32)
-    for b in range(NZ * NX):
-        before += jnp.where(sg_ref[b] < ids, 1.0, 0.0)
-    before = jnp.sum(before, axis=1, keepdims=True)
-    id_col = lax.broadcasted_iota(jnp.int32, (IDS, QT), 0).astype(F32)
-    lane = lax.broadcasted_iota(jnp.int32, (1, 128), 1)
-    lane_q = lax.broadcasted_iota(jnp.int32, (1, QT), 1)
-    half = lane < ROWS
+    shift = origin(z, y, x, c)[2]
+
+    def piece(t):
+        return tile_start(t, shift)
 
     for t in range(NQT):
-        g = t * TILE_G
-        stats = [st_ref[g + i, 0:1, :] for i in range(TILE_G)]
-        turned = [pltpu.roll(s, ROWS, 1) for s in stats]
-        lse = jnp.concatenate(
-            [jnp.where(half, stats[0], turned[1]), jnp.where(half, stats[2], turned[3])], axis=1
-        )
-        dot = jnp.concatenate(
-            [jnp.where(half, turned[0], stats[1]), jnp.where(half, turned[2], stats[3])], axis=1
-        )
-        seg = [st_ref[g + i, 1:2, :] for i in range(TILE_G)]
-        seg = jnp.concatenate(
-            [jnp.where(half, seg[0], seg[1]), jnp.where(half, seg[2], seg[3])], axis=1
-        )
-        lo = jnp.sum(jnp.where(id_col == seg, before, 0.0), axis=0, keepdims=True)
-        piece = g + lane_q // ROWS
-        rem = piece % NZ * CHUNK + query_start + lane_q % PIECE - key_start
-        hi = piece // NZ * CHUNK + jnp.clip(rem + 1, 0, CHUNK)
-        rows_ref[t, 0:1, :] = lse * LOG2E
-        rows_ref[t, 1:2, :] = dot
-        rows_ref[t, 2:3, :] = lo
-        rows_ref[t, 3:4, :] = hi.astype(F32)
-        low_ref[t] = jnp.min(lo).astype(jnp.int32)
-        high_ref[t] = jnp.max(lo).astype(jnp.int32)
+        low_ref[t] = jnp.min(rows_ref[t, 2:3, :]).astype(jnp.int32)
 
     def clear(k, carry):
         dq_acc[2 * k] = jnp.zeros((HD, QT), F32)
         dq_acc[2 * k + 1] = jnp.zeros((HD, QT), F32)
         dk_acc[k] = jnp.zeros((KT, HD), F32)
         dv_acc[k] = jnp.zeros((KT, HD), F32)
-        keys_t[k] = kv_ref[k, :, 0:HD].T
         return carry
 
     lax.fori_loop(0, NKT, clear, 0)
-    p_ref[...] = jnp.zeros((KT, QT), BF)
-    ds_ref[...] = jnp.zeros((KT, QT), BF)
+    p_ref[...] = jnp.zeros((2, KT, QT), BF)
+    ds_ref[...] = jnp.zeros((2, KT, QT), BF)
 
     def nothing(n):
         k_list[n] = 0
         t_list[n] = 0
         from_list[n] = -(1 << 20)
-        full_list[n] = 0
 
     nothing(0)
+    nothing(1)
+    lows = [low_ref[t] for t in range(NQT)]
 
     def listed(k, count):
-        ahead = k * (NZ * CHUNK) + key_start - query_start - (PIECE - 1)
-        for t in range(NQT):
+        end = 0
+        for low in lows:
+            end += jnp.where(low < (k + 1) * KT, 1, 0)
+
+        def note(t, count):
             k_list[count] = k
             t_list[count] = t
             from_list[count] = k * KT
-            whole = (high_ref[t] <= k * KT) & (
-                k * (NZ * CHUNK) + key_start + KT - 1 <= t * TILE_G * CHUNK + query_start
-            )
-            full_list[count] = jnp.where(whole, 1, 0)
-            seen = (low_ref[t] < (k + 1) * KT) & (ahead <= (t * TILE_G + TILE_G - 1) * CHUNK)
-            count += jnp.where(seen, 1, 0)
-        return count
-
-    count = lax.fori_loop(0, NKT, listed, 1)
-    nothing(count)
-
-    def work(n, masked):
+            return count + 1
+
+        return lax.fori_loop(2 * k + y // 2, end, note, count)
+
+    count = lax.fori_loop(0, NKT, listed, 2)
+    for i in range(3):
+        nothing(count + i)
+
+    def sums(n, slot):
         k, t = k_list[n], t_list[n]
-        q = qd_ref[pl.ds(t * TILE_G, TILE_G), 0].reshape(QT, HD)
-        do = qd_ref[pl.ds(t * TILE_G, TILE_G), 1].reshape(QT, HD)
-        p, ds = p_ref[...], ds_ref[...]
+        q = qd_ref[pl.ds(piece(t), TILE_G), 0].reshape(QT, HD)
+        do = qd_ref[pl.ds(piece(t), TILE_G), 1].reshape(QT, HD)
+        p, ds = p_ref[slot], ds_ref[slot]
         dv_acc[k] += jnp.dot(p, do, preferred_element_type=F32)
         dk_acc[k] += jnp.dot(ds, q, preferred_element_type=F32)
         dq_acc[t] += jnp.dot(keys_t[k], ds, preferred_element_type=F32)
-        k, t = k_list[n + 1], t_list[n + 1]
-        q = qd_ref[pl.ds(t * TILE_G, TILE_G), 0].reshape(QT, HD)
-        do = qd_ref[pl.ds(t * TILE_G, TILE_G), 1].reshape(QT, HD)
-        start = from_list[n + 1].astype(F32)
+
+    def probabilities(n, slot):
+        k, t = k_list[n], t_list[n]
+        q = qd_ref[pl.ds(piece(t), TILE_G), 0].reshape(QT, HD)
+        do = qd_ref[pl.ds(piece(t), TILE_G), 1].reshape(QT, HD)
+        start = from_list[n].astype(F32)
         low = rows_ref[t, 2:3, :] - start
         high = rows_ref[t, 3:4, :] - start
         across = (((1,), (1,)), ((), ()))
@@ -358,45 +388,28 @@
             dp = lax.dot_general(
                 kv_ref[k, part, HD:2 * HD], do, across, preferred_element_type=F32
             )
+            index = (lax.broadcasted_iota(jnp.int32, (SUB, QT), 0) + i * SUB).astype(F32)
             p = jnp.exp2(s * (SCALE * LOG2E) - rows_ref[t, 0:1, :])
-            if masked:
-                index = (lax.broadcasted_iota(jnp.int32, (SUB, QT), 0) + i * SUB).astype(F32)
-                p = jnp.where((index >= low) & (index < high), p, 0.0)
-            p_ref[part, :] = p.astype(BF)
-            ds_ref[part, :] = (p * (dp - rows_ref[t, 1:2, :])).astype(BF)
-
-    def step(n, carry):
-        whole = full_list[n + 1] == 1
-
-        @pl.when(whole)
-        def _():
-            work(n, False)
-
-        @pl.when(jnp.logical_not(whole))
-        def _():
-            work(n, True)
-
+            p = jnp.where((index >= low) & (index < high), p, 0.0)
+            p_ref[slot, part, :] = p.astype(BF)
+            ds_ref[slot, part, :] = (p * (dp - rows_ref[t, 1:2, :])).astype(BF)
+
+    def step(i, carry):
+        n = 2 * i
+        sums(n, 0)
+        sums(n + 1, 1)
+        probabilities(n + 2, 0)
+        probabilities(n + 3, 1)
         return carry
 
-    lax.fori_loop(0, count, step, 0)
-
-    def emit(k, carry):
-        dkv_ref[k, :, 0:HD] = (dk_acc[k] * SCALE).astype(BF)
-        dkv_ref[k, :, HD:2 * HD] = dv_acc[k].astype(BF)
-        for i in range(NQT // NKT):
-            t = k * (NQT // NKT) + i
-            dq = (dq_acc[t] * SCALE).T
-            dq_ref[pl.ds(t * TILE_G, TILE_G)] = dq.astype(BF).reshape(TILE_G, ROWS, HD)
-        return carry
-
-    lax.fori_loop(0, NKT, emit, 0)
+    lax.fori_loop(0, (count + 1) // 2, step, 0)
 
 
 N_REDUCE = 16 + 16 + 7 + 7 + 4 + 1 + 2 + 2 + 7
 
 
 def reduce_kernel(
-    kv_ref, dq_in, gq_ref, gk_ref, gv_ref,
+    dq_acc, dk_acc, dv_acc, gq_ref, gk_ref, gv_ref, kv_ref, dq_in,
     far, near, out_x, ring_in, ring_out, both_in, both_out, both_sum, b_far, b_near, b_out,
     q_twin, q_sum, q_far, q_near, q_out, q_send, q_back, send, recv,
 ):
@@ -409,7 +422,31 @@
     z_right, z_left = device(zp, y, x, c), device(zm, y, x, c)
     twin = device(z, y, x, 1 - c)
     planes = [(z + d) % NZ for d in range(1, NZ)]
-    greet([right, left, up, down, twin] + [device(w, y, x, c) for w in planes])
+    shift = origin(z, y, x, c)[2]
+
+    def rounded():
+        def keys_side(k, carry):
+            for i in range(NX):
+                part = pl.ds(i * TOK, TOK)
+                kv_ref[k, i, :, 0:HD] = (dk_acc[k, part] * SCALE).astype(BF)
+                kv_ref[k, i, :, HD:2 * HD] = dv_acc[k, part].astype(BF)
+            return carry
+
+        def queries_side(i, carry):
+            for j in range(2):
+                t = NQT - 1 - 2 * i - j
+                dq = (dq_acc[t] * SCALE).astype(BF).T.reshape(TILE_G, ROWS, HD)
+                for e in range(TILE_G):
+                    g = tile_start(t, shift) + e
+                    dq_in[g // 8, g // 4 % 2, g // 2 % 2, g % 2] = dq[e]
+            return carry
+
+        for g in range(TILE_G):
+            dq_in[0, 0, g // 2, g % 2] = jnp.zeros((ROWS, HD), BF)
+        lax.fori_loop(0, NQT // 2, queries_side, 0)
+        lax.fori_loop(0, NKT, keys_side, 0)
+
+    greet([right, left, up, down, twin] + [device(w, y, x, c) for w in planes], rounded)
     copies = Copies(send, recv)
     start = copies.start
     h = ROUND // 2
@@ -558,20 +595,19 @@
 
     for do, which in [
         (q_step, 0), (x_far, 0), (both, 0), (x_far, 1), (x_far, 2), (x_far, 3), (x_near, 0),
-        (x_far, 4), (x_near, 1), (x_far, 5), (both, 1), (q_step, 1), (x_sum, 0), (x_near, 2),
-        (x_far, 6), (x_near, 3), (both, 2), (q_step, 2), (x_sum, 1), (x_near, 4), (x_far, 7),
-        (x_sum, 2), (x_near, 5), (both, 3), (x_near, 6), (x_sum, 3), (x_sum, 4), (q_step, 3),
-        (both, 4), (x_near, 7), (x_sum, 5), (x_sum, 6), (both, 5), (x_sum, 7),
+        (x_far, 4), (x_far, 5), (both, 1), (q_step, 1), (x_near, 1), (x_near, 2), (x_sum, 0),
+        (x_far, 6), (x_near, 3), (x_near, 4), (x_far, 7), (both, 2), (q_step, 2), (x_near, 5),
+        (x_sum, 1), (x_sum, 2), (x_near, 6), (both, 3), (x_sum, 3), (x_sum, 4), (q_step, 3),
+        (both, 4), (x_sum, 5), (x_near, 7), (x_sum, 6), (both, 5), (x_sum, 7),
     ]:
         do(which)
     both_end()
     for copy in queue["back"]:
         copy.wait_recv()
     for w in range(NZ):
-        for head in range(GROUP):
-            gq_ref[w * PIECE:(w + 1) * PIECE, head * HD:(head + 1) * HD] = q_back[
-                w, head * PIECE:(head + 1) * PIECE
-            ]
+        for g in range(GROUP):
+            rows = slice(w * PIECE, (w + 1) * PIECE)
+            gq_ref[rows, g * HD:(g + 1) * HD] = q_back[w, g * PIECE:(g + 1) * PIECE]
     assert copies.count == N_REDUCE, copies.count
     copies.finish()
 
@@ -580,17 +616,19 @@
     hbm = pl.BlockSpec(memory_space=pltpu.HBM)
     vmem = pl.BlockSpec(memory_space=pltpu.VMEM)
 
-    kv_all, qd_all, st_all, sg_all = pl.pallas_call(
+    kv_all, qd_all, keys_t, row_data = pl.pallas_call(
         gather_kernel,
         out_shape=[
             jax.ShapeDtypeStruct((NZ, NX, TOK, 2 * HD), BF),
             jax.ShapeDtypeStruct((NZ, 2, NC, 2, 2, ROWS, HD), BF),
-            jax.ShapeDtypeStruct((NZ, 2, NC, 2, 2, 128), F32),
-            jax.ShapeDtypeStruct((NZ, NX, 1, TOK), F32),
+            jax.ShapeDtypeStruct((NKT, HD, KT), BF),
+            jax.ShapeDtypeStruct((NQT, 8, QT), F32),
         ],
         in_specs=[hbm] * 7,
         out_specs=[vmem] * 4,
         scratch_shapes=[
+            pltpu.VMEM((NZ, 2, NC, 2, 2, 128), F32),
+            pltpu.VMEM((NZ, NX, 1, TOK), F32),
             pltpu.VMEM((TOK, GROUP * HD), BF),
             pltpu.VMEM((TOK, GROUP * HD), BF),
             pltpu.VMEM((TOK, GROUP * HD), BF),
@@ -616,25 +654,19 @@
         ]
     )
 
-    dkv, dq = pl.pallas_call(
+    sums = pl.pallas_call(
         attend_kernel,
         out_shape=[
-            jax.ShapeDtypeStruct((NKT, KT, 2 * HD), BF),
-            jax.ShapeDtypeStruct((NG, ROWS, HD), BF),
+            jax.ShapeDtypeStruct((NQT, HD, QT), F32),
+            jax.ShapeDtypeStruct((NKT, KT, HD), F32),
+            jax.ShapeDtypeStruct((NKT, KT, HD), F32),
         ],
         in_specs=[vmem] * 4,
-        out_specs=[vmem] * 2,
+        out_specs=[vmem] * 3,
         scratch_shapes=[
-            pltpu.VMEM((NQT, 8, QT), F32),
-            pltpu.VMEM((NQT, HD, QT), F32),
-            pltpu.VMEM((NKT, KT, HD), F32),
-            pltpu.VMEM((NKT, KT, HD), F32),
-            pltpu.VMEM((NKT, HD, KT), BF),
-            pltpu.VMEM((KT, QT), BF),
-            pltpu.VMEM((KT, QT), BF),
+            pltpu.VMEM((2, KT, QT), BF),
+            pltpu.VMEM((2, KT, QT), BF),
             pltpu.SMEM((NQT,), jnp.int32),
-            pltpu.SMEM((NQT,), jnp.int32),
-            pltpu.SMEM((STEPS,), jnp.int32),
             pltpu.SMEM((STEPS,), jnp.int32),
             pltpu.SMEM((STEPS,), jnp.int32),
             pltpu.SMEM((STEPS,), jnp.int32),
@@ -644,8 +676,8 @@
     )(
         kv_all.reshape(NKT, KT, 2 * HD),
         qd_all.reshape(NG, 2, ROWS, HD),
-        st_all.reshape(NG, 2, 128),
-        sg_all.reshape(NZ * NX, 1, TOK),
+        keys_t,
+        row_data,
     )
 
     return pl.pallas_call(
@@ -655,9 +687,11 @@
             jax.ShapeDtypeStruct((TOK, HD), BF),
             jax.ShapeDtypeStruct((TOK, HD), BF),
         ],
-        in_specs=[vmem] * 2,
+        in_specs=[vmem] * 3,
         out_specs=[vmem] * 3,
         scratch_shapes=[
+            pltpu.VMEM((NZ, NX, TOK, 2 * HD), BF),
+            pltpu.VMEM((NZ, 2, NC, 2, ROWS, HD), BF),
             pltpu.VMEM((NZ, 2, ROUND // 2, 2 * HD), BF),
             pltpu.VMEM((NZ, 2, ROUND, 2 * HD), BF),
             pltpu.VMEM((NZ, 2, ROUND, 2 * HD), BF),
@@ -683,10 +717,7 @@
             collective_id=1, has_side_effects=True, vmem_limit_bytes=40 * 2**20
         ),
         name="reduce",
-    )(
-        dkv.reshape(NZ, NX, TOK, 2 * HD),
-        dq.reshape(NZ, 2, NC, 2, ROWS, HD),
-    )
+    )(*sums)
 
 
 def solution(mesh):

time: 83.7 us -> 80.3 us (0.959)
  Pallas kernels: 80.8 us -> 77.5 us
    pallas_call x1, Pallas kernels: 18.4 us -> 14.3 us  [body(): pl.pallas_call(attend_kernel, out_shape=[jax.ShapeDtypeStruct((NQT, HD, Q...]
where the time goes in v3:
time: 80.3 us; the launch traced here: 80 us
  Pallas kernels  77.5 us (97%)
  local copies, waits for them, and re-layouts  1.89 us (2%)
    pallas_call x1, Pallas kernels, body(): pl.pallas_call(gather_kernel, out_shape=[jax.ShapeDtypeStruct((NZ, NX, TO...  35.5 us
    pallas_call x1, Pallas kernels, body(): pl.pallas_call(reduce_kernel, out_shape=[jax.ShapeDtypeStruct((TOK, GROUP...  27.6 us
    pallas_call x1, Pallas kernels, body(): pl.pallas_call(attend_kernel, out_shape=[jax.ShapeDtypeStruct((NQT, HD, Q...  14.3 us
    unnamed x3, local copies, waits for them, and re-layouts  1.89 us

profile of v3, /device:TPU:2, one launch (start us, length us, event | category | flops | bytes accessed | tf_op | source)
XLA Modules:
  0.0 80.0 jit_solution(17358825781582232334)
XLA Ops:
  0.6 35.5 %gather.1 = (bf16[8,4,128,256]{3,2,1,0:T(8,128)(2,1)S(1)}, bf16[8,2,2,2,2,64,128]{6,5,4,3,2,1,0:T(8,128)(2,1)S(1)}, bf16[8,128,512]{2,1,0:T(8,128)(2,1)S(1)}, f32[16,8,256]{2,1,0:T(8,128)S(1)}) custom-call(bf16[128,512]{1,0:T(8,128)(2,1)} %q_in.1, bf16[128,128]{1,0:T(8,128)(2,1)} %k_in.1, bf16[128,128]{1,0:T(8,128)(2,1)} %v_in.1, bf16[128,512]{1,0:T(8,128)(2,1)} %o_in.1, ...), custom_call_target="tpu_custom_call" | custom-call | tf_op jit(solution)/shard_map/gather/pallas_call | solution.py:619
  36.2 14.3 %attend.1 = (f32[16,128,256]{2,1,0:T(8,128)S(1)}, f32[8,512,128]{2,1,0:T(8,128)S(1)}, f32[8,512,128]{2,1,0:T(8,128)S(1)}) custom-call(bf16[8,512,256]{2,1,0:T(8,128)(2,1)S(1)} %bitcast.4, bf16[64,2,64,128]{3,2,1,0:T(8,128)(2,1)S(1)} %bitcast.5, bf16[8,128,512]{2,1,0:T(8,128)(2,1)S(1)} %get-tuple-element.12.keys_t, f32[16,8,256]{2,1,0:T(8,128)S(1)} %get-tuple-element.13.rows_ref), custom_call_target="tpu_custom_call" | custom-call | tf_op jit(solution)/shard_map/attend/pallas_call | solution.py:657
  50.5 27.6 %reduce.1 = (bf16[128,512]{1,0:T(8,128)(2,1)S(1)}, bf16[128,128]{1,0:T(8,128)(2,1)S(1)}, bf16[128,128]{1,0:T(8,128)(2,1)S(1)}) custom-call(f32[16,128,256]{2,1,0:T(8,128)S(1)} %get-tuple-element.14.dq_acc, f32[8,512,128]{2,1,0:T(8,128)S(1)} %get-tuple-element.15.dk_acc, f32[8,512,128]{2,1,0:T(8,128)S(1)} %get-tuple-element.16.dv_acc), custom_call_target="tpu_custom_call" | custom-call | tf_op jit(solution)/shard_map/reduce/pallas_call | solution.py:683
  78.2 0.7 copy.13
  78.8 0.6 copy.14
  79.4 0.6 copy.15

commit v4 on v3

--- a/solution.py
+++ b/solution.py
@@ -87,7 +87,7 @@
     pl.semaphore_wait(barrier, len(peers))
 
 
-N_GATHER = 32 + 7 + 7 + 24 + 4 + 11 + 10
+N_GATHER = 34 + 9 + 7 + 24 + 4 + 11 + 10
 
 
 def gather_kernel(
@@ -129,28 +129,38 @@
     steps = [0, 1, -1, 2, -2, 3, -3, 4]
     h = TOK // 2
 
+    def block_to(d, to):
+        if d != 0:
+            src = kv_all.at[(z + NZ + d) % NZ, x]
+            return [start(src, src, to)]
+        return [
+            start(src, kv_all.at[z, x, :, pl.ds(i * HD, HD)], to)
+            for i, src in enumerate((k_in, v_in))
+        ]
+
     def ring(s):
         if 0 < s < 4:
-            hops["r", s].wait_recv()
+            for copy in hops["r", s]:
+                copy.wait_recv()
         if s < 3:
-            src = kv_all.at[(z + NZ - s) % NZ, x]
-            hops["r", s + 1] = start(src, src, z_right)
+            hops["r", s + 1] = block_to(-s, z_right)
         if s > 0:
-            hops["l", s].wait_recv()
+            for copy in hops["l", s]:
+                copy.wait_recv()
         if s < 4:
-            src = kv_all.at[(z + s) % NZ, x]
-            hops["l", s + 1] = start(src, src, z_left)
+            hops["l", s + 1] = block_to(s, z_left)
 
     def spread(d):
-        src = kv_all.at[(z + NZ + d) % NZ, x]
-        near[d] = (start(src, src, right), start(src, src, left))
+        near[d] = (block_to(d, right), block_to(d, left))
 
     def pass_on(d):
         zb = (z + NZ + d) % NZ
-        near[d][0].wait_recv()
+        for copy in near[d][0]:
+            copy.wait_recv()
         src = kv_all.at[zb, xm, pl.ds(0, h)]
         far[d] = [start(src, src, right)]
-        near[d][1].wait_recv()
+        for copy in near[d][1]:
+            copy.wait_recv()
         src = kv_all.at[zb, xp, pl.ds(h, h)]
         far[d].append(start(src, src, left))
 
@@ -247,6 +257,9 @@
         zb = (z + NZ + d) % NZ
         for copy in far[d]:
             copy.wait_recv()
+        if d == 0:
+            load[0].wait()
+            load[1].wait()
         for i in range(NX):
             keys_t[zb, :, i * TOK:(i + 1) * TOK] = kv_all[zb, i, :, 0:HD].T
 
@@ -294,8 +307,6 @@
 
         lax.fori_loop(0, NQT, one_tile, 0)
 
-    load[0].wait()
-    load[1].wait()
     for do, which in [
         (spread, 0), (ring, 0), (pack, 0), (q_send, -1), (q_share, 0), (q_send, 3), (q_send, -2),
         (ring, 1), (q_send, -3), (q_send, 1), (spread, 1), (q_send, 4), (pass_on, 0),
@@ -336,16 +347,12 @@
         return carry
 
     lax.fori_loop(0, NKT, clear, 0)
-    p_ref[...] = jnp.zeros((2, KT, QT), BF)
-    ds_ref[...] = jnp.zeros((2, KT, QT), BF)
 
     def nothing(n):
         k_list[n] = 0
         t_list[n] = 0
         from_list[n] = -(1 << 20)
 
-    nothing(0)
-    nothing(1)
     lows = [low_ref[t] for t in range(NQT)]
 
     def listed(k, count):
@@ -361,9 +368,8 @@
 
         return lax.fori_loop(2 * k + y // 2, end, note, count)
 
-    count = lax.fori_loop(0, NKT, listed, 2)
-    for i in range(3):
-        nothing(count + i)
+    count = lax.fori_loop(0, NKT, listed, 0)
+    nothing(count)
 
     def sums(n, slot):
         k, t = k_list[n], t_list[n]
@@ -402,7 +408,12 @@
         probabilities(n + 3, 1)
         return carry
 
-    lax.fori_loop(0, (count + 1) // 2, step, 0)
+    steps = (count + 1) // 2
+    probabilities(0, 0)
+    probabilities(1, 1)
+    lax.fori_loop(0, steps - 1, step, 0)
+    sums(2 * steps - 2, 0)
+    sums(2 * steps - 1, 1)
 
 
 N_REDUCE = 16 + 16 + 7 + 7 + 4 + 1 + 2 + 2 + 7

time: 80.3 us -> 79.3 us (0.988)
  Pallas kernels: 77.5 us -> 76.1 us
    pallas_call x1, Pallas kernels: 14.3 us -> 13.3 us  [body(): pl.pallas_call(attend_kernel, out_shape=[jax.ShapeDtypeStruct((NQT, HD, Q...]
where the time goes in v4:
time: 79.3 us; the launch traced here: 78.6 us
  Pallas kernels  76.1 us (96%)
  local copies, waits for them, and re-layouts  1.89 us (2%)
    pallas_call x1, Pallas kernels, body(): pl.pallas_call(gather_kernel, out_shape=[jax.ShapeDtypeStruct((NZ, NX, TO...  35.9 us
    pallas_call x1, Pallas kernels, body(): pl.pallas_call(reduce_kernel, out_shape=[jax.ShapeDtypeStruct((TOK, GROUP...  26.9 us
    pallas_call x1, Pallas kernels, body(): pl.pallas_call(attend_kernel, out_shape=[jax.ShapeDtypeStruct((NQT, HD, Q...  13.3 us
    unnamed x3, local copies, waits for them, and re-layouts  1.89 us

profile of v4, /device:TPU:2, one launch (start us, length us, event | category | flops | bytes accessed | tf_op | source)
XLA Modules:
  0.0 78.6 jit_solution(16688875605542811351)
XLA Ops:
  0.6 35.9 %gather.1 = (bf16[8,4,128,256]{3,2,1,0:T(8,128)(2,1)S(1)}, bf16[8,2,2,2,2,64,128]{6,5,4,3,2,1,0:T(8,128)(2,1)S(1)}, bf16[8,128,512]{2,1,0:T(8,128)(2,1)S(1)}, f32[16,8,256]{2,1,0:T(8,128)S(1)}) custom-call(bf16[128,512]{1,0:T(8,128)(2,1)} %q_in.1, bf16[128,128]{1,0:T(8,128)(2,1)} %k_in.1, bf16[128,128]{1,0:T(8,128)(2,1)} %v_in.1, bf16[128,512]{1,0:T(8,128)(2,1)} %o_in.1, ...), custom_call_target="tpu_custom_call" | custom-call | tf_op jit(solution)/shard_map/gather/pallas_call | solution.py:630
  36.5 13.3 %attend.1 = (f32[16,128,256]{2,1,0:T(8,128)S(1)}, f32[8,512,128]{2,1,0:T(8,128)S(1)}, f32[8,512,128]{2,1,0:T(8,128)S(1)}) custom-call(bf16[8,512,256]{2,1,0:T(8,128)(2,1)S(1)} %bitcast.4, bf16[64,2,64,128]{3,2,1,0:T(8,128)(2,1)S(1)} %bitcast.5, bf16[8,128,512]{2,1,0:T(8,128)(2,1)S(1)} %get-tuple-element.12.keys_t, f32[16,8,256]{2,1,0:T(8,128)S(1)} %get-tuple-element.13.rows_ref), custom_call_target="tpu_custom_call" | custom-call | tf_op jit(solution)/shard_map/attend/pallas_call | solution.py:668
  49.9 26.9 %reduce.1 = (bf16[128,512]{1,0:T(8,128)(2,1)S(1)}, bf16[128,128]{1,0:T(8,128)(2,1)S(1)}, bf16[128,128]{1,0:T(8,128)(2,1)S(1)}) custom-call(f32[16,128,256]{2,1,0:T(8,128)S(1)} %get-tuple-element.14.dq_acc, f32[8,512,128]{2,1,0:T(8,128)S(1)} %get-tuple-element.15.dk_acc, f32[8,512,128]{2,1,0:T(8,128)S(1)} %get-tuple-element.16.dv_acc), custom_call_target="tpu_custom_call" | custom-call | tf_op jit(solution)/shard_map/reduce/pallas_call | solution.py:694
  76.7 0.7 copy.13
  77.4 0.6 copy.14
  78.0 0.6 copy.15

commit v5 on v4

--- a/solution.py
+++ b/solution.py
@@ -20,7 +20,7 @@
 NQT = NG // TILE_G
 QT = TILE_G * ROWS
 KT = 512
-SUB = 128
+SUB = 256
 ROUND = 96
 BOTH = TOK - ROUND
 NKEY = NZ * NX * TOK
@@ -605,8 +605,8 @@
         third(n, two[n])
 
     for do, which in [
-        (q_step, 0), (x_far, 0), (both, 0), (x_far, 1), (x_far, 2), (x_far, 3), (x_near, 0),
-        (x_far, 4), (x_far, 5), (both, 1), (q_step, 1), (x_near, 1), (x_near, 2), (x_sum, 0),
+        (x_far, 0), (both, 0), (x_far, 1), (x_far, 2), (x_far, 3), (q_step, 0), (x_near, 0),
+        (x_far, 4), (x_far, 5), (both, 1), (x_near, 1), (q_step, 1), (x_near, 2), (x_sum, 0),
         (x_far, 6), (x_near, 3), (x_near, 4), (x_far, 7), (both, 2), (q_step, 2), (x_near, 5),
         (x_sum, 1), (x_sum, 2), (x_near, 6), (both, 3), (x_sum, 3), (x_sum, 4), (q_step, 3),
         (both, 4), (x_sum, 5), (x_near, 7), (x_sum, 6), (both, 5), (x_sum, 7),

time: 79.3 us -> 79.1 us (level)
    pallas_call x1, Pallas kernels: 26.9 us -> 29.1 us  [body(): pl.pallas_call(reduce_kernel, out_shape=[jax.ShapeDtypeStruct((TOK, GROUP...]
    pallas_call x1, Pallas kernels: 13.3 us -> 11.5 us  [body(): pl.pallas_call(attend_kernel, out_shape=[jax.ShapeDtypeStruct((NQT, HD, Q...]
where the time goes in v5:
time: 79.1 us; the launch traced here: 79 us
  Pallas kernels  76.5 us (97%)
  local copies, waits for them, and re-layouts  1.89 us (2%)
    pallas_call x1, Pallas kernels, body(): pl.pallas_call(gather_kernel, out_shape=[jax.ShapeDtypeStruct((NZ, NX, TO...  35.9 us
    pallas_call x1, Pallas kernels, body(): pl.pallas_call(reduce_kernel, out_shape=[jax.ShapeDtypeStruct((TOK, GROUP...  29.1 us
    pallas_call x1, Pallas kernels, body(): pl.pallas_call(attend_kernel, out_shape=[jax.ShapeDtypeStruct((NQT, HD, Q...  11.5 us
    unnamed x3, local copies, waits for them, and re-layouts  1.89 us

profile of v5, /device:TPU:2, one launch (start us, length us, event | category | flops | bytes accessed | tf_op | source)
XLA Modules:
  0.0 79.0 jit_solution(4474567732206029860)
XLA Ops:
  0.6 35.9 %gather.1 = (bf16[8,4,128,256]{3,2,1,0:T(8,128)(2,1)S(1)}, bf16[8,2,2,2,2,64,128]{6,5,4,3,2,1,0:T(8,128)(2,1)S(1)}, bf16[8,128,512]{2,1,0:T(8,128)(2,1)S(1)}, f32[16,8,256]{2,1,0:T(8,128)S(1)}) custom-call(bf16[128,512]{1,0:T(8,128)(2,1)} %q_in.1, bf16[128,128]{1,0:T(8,128)(2,1)} %k_in.1, bf16[128,128]{1,0:T(8,128)(2,1)} %v_in.1, bf16[128,512]{1,0:T(8,128)(2,1)} %o_in.1, ...), custom_call_target="tpu_custom_call" | custom-call | tf_op jit(solution)/shard_map/gather/pallas_call | solution.py:630
  36.5 11.5 %attend.1 = (f32[16,128,256]{2,1,0:T(8,128)S(1)}, f32[8,512,128]{2,1,0:T(8,128)S(1)}, f32[8,512,128]{2,1,0:T(8,128)S(1)}) custom-call(bf16[8,512,256]{2,1,0:T(8,128)(2,1)S(1)} %bitcast.4, bf16[64,2,64,128]{3,2,1,0:T(8,128)(2,1)S(1)} %bitcast.5, bf16[8,128,512]{2,1,0:T(8,128)(2,1)S(1)} %get-tuple-element.12.keys_t, f32[16,8,256]{2,1,0:T(8,128)S(1)} %get-tuple-element.13.rows_ref), custom_call_target="tpu_custom_call" | custom-call | tf_op jit(solution)/shard_map/attend/pallas_call | solution.py:668
  48.0 29.1 %reduce.1 = (bf16[128,512]{1,0:T(8,128)(2,1)S(1)}, bf16[128,128]{1,0:T(8,128)(2,1)S(1)}, bf16[128,128]{1,0:T(8,128)(2,1)S(1)}) custom-call(f32[16,128,256]{2,1,0:T(8,128)S(1)} %get-tuple-element.14.dq_acc, f32[8,512,128]{2,1,0:T(8,128)S(1)} %get-tuple-element.15.dk_acc, f32[8,512,128]{2,1,0:T(8,128)S(1)} %get-tuple-element.16.dv_acc), custom_call_target="tpu_custom_call" | custom-call | tf_op jit(solution)/shard_map/reduce/pallas_call | solution.py:694
  77.2 0.7 copy.13
  77.8 0.6 copy.14
  78.4 0.6 copy.15

commit v6 on v4

--- a/solution.py
+++ b/solution.py
@@ -20,7 +20,7 @@
 NQT = NG // TILE_G
 QT = TILE_G * ROWS
 KT = 512
-SUB = 128
+SUB = 256
 ROUND = 96
 BOTH = TOK - ROUND
 NKEY = NZ * NX * TOK
@@ -420,7 +420,7 @@
 
 
 def reduce_kernel(
-    dq_acc, dk_acc, dv_acc, gq_ref, gk_ref, gv_ref, kv_ref, dq_in,
+    dq_acc, dk_acc, dv_acc, gq_ref, gkv_ref, kv_ref, dq_in,
     far, near, out_x, ring_in, ring_out, both_in, both_out, both_sum, b_far, b_near, b_out,
     q_twin, q_sum, q_far, q_near, q_out, q_send, q_back, send, recv,
 ):
@@ -509,8 +509,7 @@
             ring[("r", 4)].wait_recv()
             ring[("l", 3)].wait_recv()
             total += ring_in[3].astype(F32) + ring_in[6].astype(F32)
-            gk_ref[0:ROUND] = total[:, 0:HD].astype(BF)
-            gv_ref[0:ROUND] = total[:, HD:2 * HD].astype(BF)
+            gkv_ref[0:ROUND] = total.astype(BF)
 
     def both(s):
         if s == 0:
@@ -553,8 +552,7 @@
         ring["n", 0].wait_recv()
         ring["n", 1].wait_recv()
         total = both_sum[x].astype(F32) + b_near[0].astype(F32) + b_near[1].astype(F32)
-        gk_ref[ROUND:TOK] = total[:, 0:HD].astype(BF)
-        gv_ref[ROUND:TOK] = total[:, HD:2 * HD].astype(BF)
+        gkv_ref[ROUND:TOK] = total.astype(BF)
 
     queue = {}
 
@@ -691,15 +689,14 @@
         row_data,
     )
 
-    return pl.pallas_call(
+    grad_q, grad_kv = pl.pallas_call(
         reduce_kernel,
         out_shape=[
             jax.ShapeDtypeStruct((TOK, GROUP * HD), BF),
-            jax.ShapeDtypeStruct((TOK, HD), BF),
-            jax.ShapeDtypeStruct((TOK, HD), BF),
+            jax.ShapeDtypeStruct((TOK, 2 * HD), BF),
         ],
         in_specs=[vmem] * 3,
-        out_specs=[vmem] * 3,
+        out_specs=[vmem] * 2,
         scratch_shapes=[
             pltpu.VMEM((NZ, NX, TOK, 2 * HD), BF),
             pltpu.VMEM((NZ, 2, NC, 2, ROWS, HD), BF),
@@ -729,6 +726,7 @@
         ),
         name="reduce",
     )(*sums)
+    return grad_q, grad_kv[:, :HD], grad_kv[:, HD:]
 
 
 def solution(mesh):

time: 79.3 us -> 78.5 us (0.990)
    unnamed x3 -> x1, local copies, waits for them, and re-layouts: 1.89 us -> 0.65 us
where the time goes in v6:
time: 78.5 us; the launch traced here: 78.3 us
  Pallas kernels  76.4 us (97%)
  local copies, waits for them, and re-layouts  1.29 us (2%)
    pallas_call x1, Pallas kernels, body(): pl.pallas_call(gather_kernel, out_shape=[jax.ShapeDtypeStruct((NZ, NX, TO...  35.9 us
    pallas_call x1, Pallas kernels, body(): pl.pallas_call(reduce_kernel, out_shape=[jax.ShapeDtypeStruct((TOK, GROUP...  27.3 us
    pallas_call x1, Pallas kernels, body(): pl.pallas_call(attend_kernel, out_shape=[jax.ShapeDtypeStruct((NQT, HD, Q...  13.2 us

profile of v6, /device:TPU:2, one launch (start us, length us, event | category | flops | bytes accessed | tf_op | source)
XLA Modules:
  0.0 78.3 jit_solution(341503535730957606)
XLA Ops:
  0.6 35.9 %gather.1 = (bf16[8,4,128,256]{3,2,1,0:T(8,128)(2,1)S(1)}, bf16[8,2,2,2,2,64,128]{6,5,4,3,2,1,0:T(8,128)(2,1)S(1)}, bf16[8,128,512]{2,1,0:T(8,128)(2,1)S(1)}, f32[16,8,256]{2,1,0:T(8,128)S(1)}) custom-call(bf16[128,512]{1,0:T(8,128)(2,1)} %q_in.1, bf16[128,128]{1,0:T(8,128)(2,1)} %k_in.1, bf16[128,128]{1,0:T(8,128)(2,1)} %v_in.1, bf16[128,512]{1,0:T(8,128)(2,1)} %o_in.1, ...), custom_call_target="tpu_custom_call" | custom-call | tf_op jit(solution)/shard_map/gather/pallas_call | solution.py:628
  36.5 13.2 %attend.1 = (f32[16,128,256]{2,1,0:T(8,128)S(1)}, f32[8,512,128]{2,1,0:T(8,128)S(1)}, f32[8,512,128]{2,1,0:T(8,128)S(1)}) custom-call(bf16[8,512,256]{2,1,0:T(8,128)(2,1)S(1)} %bitcast.4, bf16[64,2,64,128]{3,2,1,0:T(8,128)(2,1)S(1)} %bitcast.5, bf16[8,128,512]{2,1,0:T(8,128)(2,1)S(1)} %get-tuple-element.14.keys_t, f32[16,8,256]{2,1,0:T(8,128)S(1)} %get-tuple-element.15.rows_ref), custom_call_target="tpu_custom_call" | custom-call | tf_op jit(solution)/shard_map/attend/pallas_call | solution.py:666
  49.7 27.3 %reduce.1 = (bf16[128,512]{1,0:T(8,128)(2,1)S(1)}, bf16[128,256]{1,0:T(8,128)(2,1)S(1)}) custom-call(f32[16,128,256]{2,1,0:T(8,128)S(1)} %get-tuple-element.16.dq_acc, f32[8,512,128]{2,1,0:T(8,128)S(1)} %get-tuple-element.17.dk_acc, f32[8,512,128]{2,1,0:T(8,128)S(1)} %get-tuple-element.18.dv_acc), custom_call_target="tpu_custom_call" | custom-call | tf_op jit(solution)/shard_map/reduce/pallas_call | solution.py:692
  77.1 0.6 fusion
  77.7 0.7 copy.11
